TPU v7x, 256 devices: a whole 4x4x8 slice. The times are simulated.
256 devices in a mesh: lat: 32 (over z_hi, y, core), lon: 8 (over x, z_lo).
Axes of the slice: x: 4, y: 4, z: 8 (z_hi: 4, z_lo: 2; z = z_hi * 2 + z_lo), core: 2. Of those that a mesh axis runs over, the one named last changes fastest.
Arguments:
- grid_cot: float32 [4, 64, 16, 5120], P(None, 'lat', None, 'lon'), may hold values from -6 to 6
- weights: bfloat16 [64, 16, 4, 5120], P('lat', None, None, 'lon'), may hold values from 0 to 1
- offsets: int32 [64, 16, 2, 5120], P('lat', None, None, 'lon'), may hold values from -4 to 3, as said below
- lat_points: int32 [64], P('lat'), may hold values from 1280 to 5120
- slot_mode: int32 [1280], replicated, may hold values from 0 to 1279, each once
- legendre: bfloat16 [1280, 64, 1280], P('lat'), may hold values from -0.009765625 to 0.009765625
Outputs:
- spectral_cot: bfloat16 [1280, 2, 4, 16, 1280], P('lat', None, None, 'lon')
Inputs may be any that keep to these rules, and one draw needn't show every extreme that they name: offsets[i, v, 0, j] is -1 or 0 and rows i + offsets[i, v, 0, j] and that plus 1 lie in the grid; offsets[i, v, 1, j] lies in -4 to 3. `slot_mode`: a permutation of the wavenumbers; the device with index k along lat owns slots k * 1280 / 32 onward.
All inputs are finite; a program needn't handle non-finite values.
Results may differ from a plain program's by a relative error of at most 0.005.
Values may be sent and summed in bfloat16 or wider, within the bound.
No kernel may reach another device: no remote copies, remote signals or barrier semaphores. Data moves between devices by JAX's collectives and lax.ppermute only.
A program may use at most 64 MiB of HBM per device.

v0:
```python
import jax
import jax.numpy as jnp
from jax import lax
from jax.sharding import PartitionSpec as P

M = 1280
NL = 1280
REACH_LON = 4


def padded(value, sides, width, wrap):
    for axis, dim in sides:
        size, length = (lax.axis_size(axis), value.shape[dim])
        up = [(i, (i + 1) % size) for i in range(size if wrap else size - 1)]
        down = [(j, i) for i, j in up]
        last = lax.slice_in_dim(value, length - width, length, axis=dim)
        first = lax.slice_in_dim(value, 0, width, axis=dim)
        before = lax.ppermute(last, axis, up)
        after = lax.ppermute(first, axis, down)
        value = jnp.concatenate([before, value, after], axis=dim)
    return value


def fourier_table(col_count, modes, circle):
    longitude = jnp.arange(col_count, dtype=jnp.int32)
    wavenumber = jnp.arange(modes, dtype=jnp.int32)
    phase = longitude[:, None] * wavenumber[None, :] % circle
    angle = 2.0 * jnp.pi / circle * phase.astype(jnp.float32)
    factor = jnp.where(wavenumber == 0, 1.0, 2.0).astype(jnp.float32)
    return jnp.concatenate([factor * jnp.cos(angle), -factor * jnp.sin(angle)], axis=1)


def deposit_local(grid_cot, weights, offsets, reach):
    fields, lat_rows, levels, lon_cols = grid_cot.shape
    north_off = offsets[None, :, :, 0, :]
    east_off = offsets[None, :, :, 1, :]
    corner = []
    for corner_id in range(4):
        corner.append(grid_cot * weights[None, :, :, corner_id, :].astype(jnp.float32))
    zeros = jnp.zeros_like(grid_cot)
    south_sel = north_off == -1
    here_sel = north_off == 0
    by_row = {}
    by_row[-1] = (jnp.where(south_sel, corner[0], zeros), jnp.where(south_sel, corner[1], zeros))
    by_row[0] = (
        jnp.where(here_sel, corner[0], zeros) + jnp.where(south_sel, corner[2], zeros),
        jnp.where(here_sel, corner[1], zeros) + jnp.where(south_sel, corner[3], zeros),
    )
    by_row[1] = (jnp.where(here_sel, corner[2], zeros), jnp.where(here_sel, corner[3], zeros))
    deposit = jnp.zeros((fields, lat_rows + 2, levels, lon_cols + 2 * reach), jnp.float32)
    for row_shift in (-1, 0, 1):
        west_part, east_part = by_row[row_shift]
        for col_shift in range(-reach, reach + 1):
            piece = jnp.where(east_off == col_shift, west_part, zeros)
            piece = piece + jnp.where(east_off == col_shift - 1, east_part, zeros)
            deposit = deposit + jnp.pad(
                piece,
                (
                    (0, 0),
                    (row_shift + 1, 1 - row_shift),
                    (0, 0),
                    (col_shift + reach, reach - col_shift),
                ),
            )
    return deposit


def per_device(grid_cot, weights, offsets, lat_points, slot_mode, legendre):
    fields, lat_rows, levels, lon_cols = grid_cot.shape
    deposit = deposit_local(grid_cot, weights, offsets, REACH_LON)
    widened = padded(deposit, (("lon", 3),), REACH_LON, True)
    folded = widened[:, :, :, 2 * REACH_LON : 2 * REACH_LON + lon_cols]
    folded = folded.at[:, :, :, :REACH_LON].add(widened[:, :, :, :REACH_LON])
    folded = folded.at[:, :, :, lon_cols - REACH_LON :].add(
        widened[:, :, :, lon_cols + 3 * REACH_LON :]
    )
    stacked = padded(folded, (("lat", 1),), 1, False)
    adjoint_grid = stacked[:, 2 : lat_rows + 2]
    adjoint_grid = adjoint_grid.at[:, 0].add(stacked[:, 0])
    adjoint_grid = adjoint_grid.at[:, lat_rows - 1].add(stacked[:, lat_rows + 3])
    sectors = lax.axis_size("lon")
    circle = lon_cols * sectors
    full_circle = lax.all_to_all(adjoint_grid, "lon", split_axis=2, concat_axis=3, tiled=True)
    base_table = fourier_table(lon_cols, M, circle)
    wavenumber_all = jnp.arange(M, dtype=jnp.int32)

    def add_sector(sector, running):
        first_col = sector * lon_cols
        sector_grid = lax.dynamic_slice_in_dim(full_circle, first_col, lon_cols, 3)
        terms = jnp.dot(
            sector_grid,
            base_table,
            precision=lax.Precision.HIGHEST,
            preferred_element_type=jnp.float32,
        )
        real_part = terms[..., :M]
        imag_part = terms[..., M:]
        phase = first_col * wavenumber_all % circle
        angle = 2.0 * jnp.pi / circle * phase.astype(jnp.float32)
        cosine = jnp.cos(angle)
        sine = jnp.sin(angle)
        turned_real = cosine * real_part + sine * imag_part
        turned_imag = cosine * imag_part - sine * real_part
        return running + jnp.concatenate([turned_real, turned_imag], axis=3)

    initial = jnp.zeros((fields, lat_rows, levels // sectors, 2 * M), jnp.float32)
    spectra = lax.fori_loop(0, sectors, add_sector, initial)
    spectra = spectra.reshape(fields, lat_rows, levels // sectors, 2, M)
    wavenumber = jnp.arange(M, dtype=jnp.int32)
    mode_mask = (2 * wavenumber[None, :] < lat_points[:, None]).astype(jnp.float32)
    masked = (spectra * mode_mask[None, :, None, None, :]).astype(jnp.bfloat16)
    ordered = jnp.take(masked, slot_mode, axis=4)
    per_owner = M // lax.axis_size("lat")
    first_slot = lax.axis_index("lat") * per_owner
    my_modes = lax.dynamic_slice_in_dim(slot_mode, first_slot, per_owner, 0)
    degree = jnp.arange(NL, dtype=jnp.int32)
    degree_mask = (degree[None, :] >= my_modes[:, None]).astype(jnp.float32)
    result = jnp.einsum(
        "stl,ftvrs->srfvl",
        legendre,
        lax.all_to_all(ordered, "lat", split_axis=4, concat_axis=1, tiled=True),
        preferred_element_type=jnp.float32,
    )
    return (result * degree_mask[:, None, None, None, :]).astype(jnp.bfloat16)


def solution(mesh):
    placed = (
        P(None, "lat", None, "lon"),
        P("lat", None, None, "lon"),
        P("lat", None, None, "lon"),
        P("lat"),
        P(),
        P("lat", None, None),
    )
    return jax.shard_map(
        per_device,
        mesh=mesh,
        in_specs=placed,
        out_specs=P("lat", None, None, "lon", None),
        check_vma=False,
    )
```

profile of v0, /device:TPU:1, one launch (start us, length us, event | category | flops | bytes accessed | tf_op | source)
XLA Modules:
  0.0 178.1 jit_solution(10001661552997058494)
XLA Ops:
  0.0 1.1 fusion.43
  1.1 1.5 fusion.42
  2.7 0.1 compare_bitcast_fusion.8
  2.9 1.4 select_add_fusion.28
  4.3 1.2 select_add_fusion.7
  5.5 3.3 %pad_add_fusion = f32[4,4,16,648]{3,2,1,0:T(8,128)S(1)} fusion(f32[4,2,16,640]{3,2,1,0:T(8,128)S(1)} %get-tuple-element.250, f32[4,2,16,640]{3,2,1,0:T(8,128)S(1)} %get-tuple-element.249, f32[4,2,16,640]{3,2,1,0:T(8,128)S(1)} %get-tuple-element.248, f32[4,2,16,640]{3,2,1,0:T(8,128)S(1)} %get-tuple-element.247, f32[4,2,16,640]{3,2,1,0:T(8,128)S(1)} %get-tuple-element.246, ...), kind=kLoop, calls=%fused_computation.36 | loop fusion | flops 4313088 | bytes 9510912 | tf_op jit(solution)/shard_map/add | solution.py:56
  8.7 0.7 fusion.40
  9.4 2.5 %collective-permute-start = (f32[4,4,16,4]{3,2,1,0:T(8,128)S(1)}, f32[4,4,16,4]{3,2,1,0:T(8,128)S(1)}, u32[]{:S(2)}, u32[]{:S(2)}) collective-permute-start(f32[4,4,16,4]{3,2,1,0:T(8,128)S(1)} %get-tuple-element.226), channel_id=1, source_target_pairs={{0,1},{1,2},{2,3},{3,4},{4,5},{5,6},{6,7},{7,0},{8,9},{9,10},{10,1... | collective-permute-start | bytes 12296 | tf_op jit(solution)/shard_map/ppermute | solution.py:18
  11.9 2.2 %collective-permute-start.1 = (f32[4,4,16,4]{3,2,1,0:T(8,128)}, f32[4,4,16,4]{3,2,1,0:T(8,128)}, u32[]{:S(2)}, u32[]{:S(2)}) collective-permute-start(f32[4,4,16,4]{3,2,1,0:T(8,128)} %get-tuple-element.225), channel_id=1, source_target_pairs={{1,0},{2,1},{3,2},{4,3},{5,4},{6,5},{7,6},{0,7},{9,8},{10,9},{11,1... | collective-permute-start | bytes 12296 | tf_op jit(solution)/shard_map/ppermute | solution.py:19
  14.1 14.4 %sine_multiply_fusion = (f32[640,1280]{1,0:T(8,128)S(1)}, f32[640,1280]{1,0:T(8,128)}) fusion(f32[1280]{0:T(1024)S(1)} %fusion.39, f32[1280]{0:T(1024)S(1)} %fusion.38), kind=kLoop, calls=%fused_computation.27 | loop fusion | flops 9011200 | bytes 6563840 | tf_op jit(solution)/shard_map/mul | solution.py:30
  28.5 0.1 compare_convert_fusion
  28.6 1.1 slice.192
  29.7 0.1 slice_add_fusion.3
  29.8 1.7 scatter-add.14
  31.5 1.1 slice_add_fusion.2
  32.6 3.3 %scatter-add.15 = f32[4,4,16,640]{3,2,1,0:T(8,128)} dynamic-update-slice(f32[4,4,16,640]{3,2,1,0:T(8,128)} %scatter-add.14, f32[4,4,16,4]{3,2,1,0:T(8,128)S(1)} %slice_add_fusion.2, s32[]{:T(128)} %constant.214.clone.1, s32[]{:T(128)} %constant.214.clone.1, s32[]{:T(128)} %constant.214.clone.1, s32[]{:T(128)} %constant.227.clone.1) | dynamic-update-slice | bytes 8196 | tf_op jit(solution)/shard_map/scatter-add | solution.py:74
  35.9 1.0 fusion.41
  36.9 4.1 %collective-permute-start.2 = (f32[4,1,16,640]{3,2,1,0:T(8,128)S(1)}, f32[4,1,16,640]{3,2,1,0:T(8,128)S(1)}, u32[]{:S(2)}, u32[]{:S(2)}) collective-permute-start(f32[4,1,16,640]{3,2,1,0:T(8,128)S(1)} %get-tuple-element.252), channel_id=1, source_target_pairs={{0,8},{8,16},{16,24},{24,32},{32,40},{40,48},{48,56},{56,64},{64,7... | collective-permute-start | bytes 491528 | tf_op jit(solution)/shard_map/ppermute | solution.py:18
  41.0 1.0 slice.197
  42.0 1.9 %collective-permute-start.3 = (f32[4,1,16,640]{3,2,1,0:T(8,128)S(1)}, f32[4,1,16,640]{3,2,1,0:T(8,128)S(1)}, u32[]{:S(2)}, u32[]{:S(2)}) collective-permute-start(f32[4,1,16,640]{3,2,1,0:T(8,128)S(1)} %get-tuple-element.251), channel_id=1, source_target_pairs={{8,0},{16,8},{24,16},{32,24},{40,32},{48,40},{56,48},{64,56},{72,6... | collective-permute-start | bytes 491528 | tf_op jit(solution)/shard_map/ppermute | solution.py:19
  43.9 1.0 fusion.33
  44.9 3.7 %collective-permute-done.3 = f32[4,1,16,640]{3,2,1,0:T(8,128)S(1)} collective-permute-done((f32[4,1,16,640]{3,2,1,0:T(8,128)S(1)}, f32[4,1,16,640]{3,2,1,0:T(8,128)S(1)}, u32[]{:S(2)}, u32[]{:S(2)}) %collective-permute-start.3) | collective-permute-done | bytes 163872 | tf_op jit(solution)/shard_map/ppermute | solution.py:19
  48.7 0.9 copy.86
  49.6 4.3 %all-to-all-start = ((f32[4,2,16,640]{3,0,1,2:T(4,128)}), f32[4,2,16,640]{3,0,1,2:T(4,128)}, u32[]{:S(2)}, u32[]{:S(2)}) async-start(f32[4,2,16,640]{3,0,1,2:T(4,128)} %copy.86), calls=%async_computation | async-start | bytes 655360 | tf_op jit(solution)/shard_map/all_to_all | solution.py:83
  53.9 0.1 dynamic_slice.13
  54.0 5.6 %pad_maximum_fusion = f32[640,2560]{1,0:T(8,128)} fusion(f32[640,1280]{1,0:T(8,128)S(1)} %get-tuple-element.299, f32[640,1280]{1,0:T(8,128)} %get-tuple-element.300), kind=kLoop, calls=%fused_computation.19 | loop fusion | flops 1638400 | bytes 13107200 | tf_op jit(solution)/shard_map/concatenate | solution.py:30
  59.6 0.6 all-to-all-done
  60.2 1.1 copy.87
  61.3 0.1 all_to_all.29
  61.4 52.0 %while.20 = (s32[]{:T(128)}, f32[4,2,2,2560]{3,0,2,1:T(4,128)S(1)}, f32[4,2,2,5120]{3,0,2,1:T(4,128)S(1)}, f32[640,2560]{1,0:T(8,128)}, s32[]{:T(128)}, /*index=5*/s32[]{:T(128)}, s32[]{:T(128)}, s32[]{:T(128)}) while((s32[]{:T(128)}, f32[4,2,2,2560]{3,0,2,1:T(4,128)S(1)}, f32[4,2,2,5120]{3,0,2,1:T(4,128)S(1)}, ...), condition=%wide.region_1.2_spmd.clone, body=%wide.region_0.1_spmd.clone.sunk | while | flops 314830080 | bytes 7598229 | solution.py:107
  61.4 6.3 %fusion.52 = f32[4,2,2,2560]{3,0,2,1:T(4,128)S(1)} fusion(f32[640,2560]{1,0:T(8,128)} %get-tuple-element.353, f32[4,2,2,5120]{3,0,2,1:T(4,128)S(1)} %get-tuple-element.352, s32[]{:T(128)S(6)} %select_n.434), kind=kOutput, calls=%fused_computation.2.clone.1 | convolution fusion | flops 314572800 | bytes 6758404 | tf_op jit(solution)/shard_map/while/body/eval_jaxpr/dot_general | solution.py:90
  67.7 0.1 fusion.53
  67.8 0.1 maximum_add_fusion.2
  67.9 6.3 %fusion.52 = f32[4,2,2,2560]{3,0,2,1:T(4,128)S(1)} fusion(f32[640,2560]{1,0:T(8,128)} %get-tuple-element.353, f32[4,2,2,5120]{3,0,2,1:T(4,128)S(1)} %get-tuple-element.352, s32[]{:T(128)S(6)} %select_n.434), kind=kOutput, calls=%fused_computation.2.clone.1 | convolution fusion | flops 314572800 | bytes 6758404 | tf_op jit(solution)/shard_map/while/body/eval_jaxpr/dot_general | solution.py:90
  74.2 0.1 fusion.53
  74.3 0.1 maximum_add_fusion.2
  74.4 6.3 %fusion.52 = f32[4,2,2,2560]{3,0,2,1:T(4,128)S(1)} fusion(f32[640,2560]{1,0:T(8,128)} %get-tuple-element.353, f32[4,2,2,5120]{3,0,2,1:T(4,128)S(1)} %get-tuple-element.352, s32[]{:T(128)S(6)} %select_n.434), kind=kOutput, calls=%fused_computation.2.clone.1 | convolution fusion | flops 314572800 | bytes 6758404 | tf_op jit(solution)/shard_map/while/body/eval_jaxpr/dot_general | solution.py:90
  80.7 0.1 fusion.53
  80.8 0.1 maximum_add_fusion.2
  80.9 6.3 %fusion.52 = f32[4,2,2,2560]{3,0,2,1:T(4,128)S(1)} fusion(f32[640,2560]{1,0:T(8,128)} %get-tuple-element.353, f32[4,2,2,5120]{3,0,2,1:T(4,128)S(1)} %get-tuple-element.352, s32[]{:T(128)S(6)} %select_n.434), kind=kOutput, calls=%fused_computation.2.clone.1 | convolution fusion | flops 314572800 | bytes 6758404 | tf_op jit(solution)/shard_map/while/body/eval_jaxpr/dot_general | solution.py:90
  87.2 0.1 fusion.53
  87.3 0.1 maximum_add_fusion.2
  87.4 6.3 %fusion.52 = f32[4,2,2,2560]{3,0,2,1:T(4,128)S(1)} fusion(f32[640,2560]{1,0:T(8,128)} %get-tuple-element.353, f32[4,2,2,5120]{3,0,2,1:T(4,128)S(1)} %get-tuple-element.352, s32[]{:T(128)S(6)} %select_n.434), kind=kOutput, calls=%fused_computation.2.clone.1 | convolution fusion | flops 314572800 | bytes 6758404 | tf_op jit(solution)/shard_map/while/body/eval_jaxpr/dot_general | solution.py:90
  93.8 0.1 maximum_add_fusion.2
  93.9 6.3 %fusion.52 = f32[4,2,2,2560]{3,0,2,1:T(4,128)S(1)} fusion(f32[640,2560]{1,0:T(8,128)} %get-tuple-element.353, f32[4,2,2,5120]{3,0,2,1:T(4,128)S(1)} %get-tuple-element.352, s32[]{:T(128)S(6)} %select_n.434), kind=kOutput, calls=%fused_computation.2.clone.1 | convolution fusion | flops 314572800 | bytes 6758404 | tf_op jit(solution)/shard_map/while/body/eval_jaxpr/dot_general | solution.py:90
  100.3 0.1 maximum_add_fusion.2
  100.4 6.3 %fusion.52 = f32[4,2,2,2560]{3,0,2,1:T(4,128)S(1)} fusion(f32[640,2560]{1,0:T(8,128)} %get-tuple-element.353, f32[4,2,2,5120]{3,0,2,1:T(4,128)S(1)} %get-tuple-element.352, s32[]{:T(128)S(6)} %select_n.434), kind=kOutput, calls=%fused_computation.2.clone.1 | convolution fusion | flops 314572800 | bytes 6758404 | tf_op jit(solution)/shard_map/while/body/eval_jaxpr/dot_general | solution.py:90
  106.7 0.1 fusion.53
  106.8 0.1 maximum_add_fusion.2
  106.9 6.3 %fusion.52 = f32[4,2,2,2560]{3,0,2,1:T(4,128)S(1)} fusion(f32[640,2560]{1,0:T(8,128)} %get-tuple-element.353, f32[4,2,2,5120]{3,0,2,1:T(4,128)S(1)} %get-tuple-element.352, s32[]{:T(128)S(6)} %select_n.434), kind=kOutput, calls=%fused_computation.2.clone.1 | convolution fusion | flops 314572800 | bytes 6758404 | tf_op jit(solution)/shard_map/while/body/eval_jaxpr/dot_general | solution.py:90
  113.3 0.1 maximum_add_fusion.2
  113.4 2.1 %copy.90 = bf16[4,2,2,2,1280]{0,3,4,2,1:T(2,128)(2,1)S(1)} copy(bf16[4,2,2,2,1280]{4,0,3,2,1:T(4,128)(2,1)S(1)} %multiply_convert_fusion) | data formatting | bytes 163840 | tf_op jit(solution)/shard_map/convert_element_type | solution.py:111
  115.6 9.3 %gather_fusion = bf16[1280,4,2,2,2]{1,4,3,2,0:T(2,128)(2,1)} fusion(bf16[4,2,2,2,1280]{0,3,4,2,1:T(2,128)(2,1)S(1)} %copy.90, s32[2048]{0:T(1024)S(1)} %pad_clamp_fusion), kind=kCustom, calls=%fused_computation | custom fusion | bytes 168960 | tf_op jit(solution)/shard_map/jit(_take)/gather | solution.py:112
  124.8 6.3 %fusion.44 = bf16[1280,2,2,2,4]{4,3,2,1,0:T(2,128)(2,1)S(1)} fusion(bf16[1280,4,2,2,2]{1,4,3,2,0:T(2,128)(2,1)} %gather_fusion, pred[1280]{0:T(1024)(128)(4,1)S(1)} %compare_and_fusion), kind=kLoop, calls=%fused_computation.111 | loop fusion | flops 40960 | bytes 165120
  131.1 5.7 %reshape.384 = bf16[32,2,640]{2,1,0:T(2,128)(2,1)} reshape(bf16[1280,2,2,2,4]{4,3,2,1,0:T(2,128)(2,1)S(1)} %fusion.44) | data formatting | bytes 163840
  136.8 14.2 %all-to-all-start.1 = ((bf16[32,2,640]{2,1,0:T(2,128)(2,1)}), bf16[32,2,640]{2,1,0:T(2,128)(2,1)S(1)}, u32[]{:S(2)}, u32[]{:S(2)}) async-start(bf16[32,2,640]{2,1,0:T(2,128)(2,1)} %reshape.384), calls=%async_computation.1 | async-start | bytes 163840 | tf_op jit(solution)/shard_map/all_to_all | solution.py:121
  151.1 0.1 fusion.31
  151.2 10.0 %all-to-all-done.1 = bf16[32,2,640]{2,1,0:T(2,128)(2,1)S(1)} async-done(((bf16[32,2,640]{2,1,0:T(2,128)(2,1)}), bf16[32,2,640]{2,1,0:T(2,128)(2,1)S(1)}, u32[]{:S(2)}, u32[]{:S(2)}) %all-to-all-start.1) | async-done | bytes 81952 | tf_op jit(solution)/shard_map/all_to_all | solution.py:121
  161.2 5.6 %reshape.385 = bf16[1280,2,2,2,4]{4,3,2,1,0:T(2,128)(2,1)S(1)} reshape(bf16[32,2,640]{2,1,0:T(2,128)(2,1)S(1)} %all-to-all-done.1) | data formatting | bytes 163840
  166.8 4.5 %copy.99 = bf16[4,2,2,2,32,40]{5,4,3,2,1,0:T(8,128)(2,1)S(1)} copy(bf16[4,2,2,2,32,40]{0,3,2,1,5,4:T(2,128)(2,1)S(1)} %bitcast.83) | data formatting | bytes 163840 | tf_op jit(solution)/shard_map/all_to_all | solution.py:121
  171.3 0.3 copy.92
  171.5 0.2 copy.93
  171.7 3.9 %fusion.27 = bf16[40,2,4,2,1280]{4,2,1,3,0:T(4,128)(2,1)S(1)} fusion(bf16[4,64,2,2,40]{1,0,3,2,4:T(4,128)(2,1)S(1)} %copy.93, bf16[40,64,1280]{2,1,0:T(8,128)(2,1)} %param.21, f32[40,1280]{1,0:T(8,128)S(1)} %fusion.31), kind=kOutput, calls=%fused_computation.34 | convolution fusion | flops 106496000 | bytes 8478720 | tf_op jit(solution)/shard_map/stl,ftvrs->srfvl/dot_general | solution.py:118
  175.6 2.5 %copy.94 = bf16[40,2,4,2,1280]{4,3,2,1,0:T(2,128)(2,1)} copy(bf16[40,2,4,2,1280]{4,2,1,3,0:T(4,128)(2,1)S(1)} %fusion.27) | data formatting | bytes 3276800 | tf_op jit(solution)/shard_map/convert_element_type | solution.py:124
  (29 shorter events, 0.7 us)
Async XLA Ops:
  9.4 20.3 %collective-permute-start = (f32[4,4,16,4]{3,2,1,0:T(8,128)S(1)}, f32[4,4,16,4]{3,2,1,0:T(8,128)S(1)}, u32[]{:S(2)}, u32[]{:S(2)}) collective-permute-start(f32[4,4,16,4]{3,2,1,0:T(8,128)S(1)} %get-tuple-element.226), channel_id=1, source_target_pairs={{0,1},{1,2},{2,3},{3,4},{4,5},{5,6},{6,7},{7,0},{8,9},{9,10},{10,1... | collective-permute-start | bytes 12296 | tf_op jit(solution)/shard_map/ppermute | solution.py:18
  11.9 19.6 %collective-permute-start.1 = (f32[4,4,16,4]{3,2,1,0:T(8,128)}, f32[4,4,16,4]{3,2,1,0:T(8,128)}, u32[]{:S(2)}, u32[]{:S(2)}) collective-permute-start(f32[4,4,16,4]{3,2,1,0:T(8,128)} %get-tuple-element.225), channel_id=1, source_target_pairs={{1,0},{2,1},{3,2},{4,3},{5,4},{6,5},{7,6},{0,7},{9,8},{10,9},{11,1... | collective-permute-start | bytes 12296 | tf_op jit(solution)/shard_map/ppermute | solution.py:19
  14.1 14.4 %copy-start.1 = (s32[2]{0:T(128)S(1)}, s32[2]{0:T(128)}, u32[]{:S(2)}) copy-start(s32[2]{0:T(128)} %param.19) | copy-start | bytes 28
  14.1 14.5 %copy-start = (s32[1280]{0:T(1024)S(1)}, s32[1280]{0:T(1024)}, u32[]{:S(2)}) copy-start(s32[1280]{0:T(1024)} %param.20) | copy-start | bytes 15364
  36.9 7.0 %collective-permute-start.2 = (f32[4,1,16,640]{3,2,1,0:T(8,128)S(1)}, f32[4,1,16,640]{3,2,1,0:T(8,128)S(1)}, u32[]{:S(2)}, u32[]{:S(2)}) collective-permute-start(f32[4,1,16,640]{3,2,1,0:T(8,128)S(1)} %get-tuple-element.252), channel_id=1, source_target_pairs={{0,8},{8,16},{16,24},{24,32},{32,40},{40,48},{48,56},{56,64},{64,7... | collective-permute-start | bytes 491528 | tf_op jit(solution)/shard_map/ppermute | solution.py:18
  42.0 6.6 %collective-permute-start.3 = (f32[4,1,16,640]{3,2,1,0:T(8,128)S(1)}, f32[4,1,16,640]{3,2,1,0:T(8,128)S(1)}, u32[]{:S(2)}, u32[]{:S(2)}) collective-permute-start(f32[4,1,16,640]{3,2,1,0:T(8,128)S(1)} %get-tuple-element.251), channel_id=1, source_target_pairs={{8,0},{16,8},{24,16},{32,24},{40,32},{48,40},{56,48},{64,56},{72,6... | collective-permute-start | bytes 491528 | tf_op jit(solution)/shard_map/ppermute | solution.py:19
  49.6 10.6 %all-to-all-start = ((f32[4,2,16,640]{3,0,1,2:T(4,128)}), f32[4,2,16,640]{3,0,1,2:T(4,128)}, u32[]{:S(2)}, u32[]{:S(2)}) async-start(f32[4,2,16,640]{3,0,1,2:T(4,128)} %copy.86), calls=%async_computation | async-start | bytes 655360 | tf_op jit(solution)/shard_map/all_to_all | solution.py:83
  136.8 24.3 %all-to-all-start.1 = ((bf16[32,2,640]{2,1,0:T(2,128)(2,1)}), bf16[32,2,640]{2,1,0:T(2,128)(2,1)S(1)}, u32[]{:S(2)}, u32[]{:S(2)}) async-start(bf16[32,2,640]{2,1,0:T(2,128)(2,1)} %reshape.384), calls=%async_computation.1 | async-start | bytes 163840 | tf_op jit(solution)/shard_map/all_to_all | solution.py:121
where the time goes:
time: 179 us; the launch traced here: 178 us
  matrix products  54 us (30%)
  local copies, waits for them, and re-layouts  43.8 us (24%)
  other arithmetic  36.2 us (20%)
  starting transfers between devices  29.1 us (16%)
  waiting for transfers between devices  14.4 us (8%)
    dot_general x8, matrix products, add_sector(): jnp.dot(sector_grid, base_table, precision=lax.Precision.HIGHEST, preferr...  50.1 us
    mul x1, other arithmetic, fourier_table(): -factor * jnp.sin(angle)  14.4 us
    all_to_all x1, starting transfers between devices, per_device(): lax.all_to_all(ordered, 'lat', split_axis=4, concat_axis=1, tiled=True)  14.2 us
    unnamed x6, local copies, waits for them, and re-layouts  11.3 us
    all_to_all x1, waiting for transfers between devices, per_device(): lax.all_to_all(ordered, 'lat', split_axis=4, concat_axis=1, tiled=True)  10 us
    gather x1, local copies, waits for them, and re-layouts, per_device(): ordered = jnp.take(masked, slot_mode, axis=4)  9.28 us
    ppermute x2, starting transfers between devices, padded(): before = lax.ppermute(last, axis, up)  6.53 us
    unnamed x2, other arithmetic  6.29 us
  transfers between devices with their start and end apart: 6, of which 3 were waited for; matrix products, arithmetic and copies ran while one was open for 14% of the time, Pallas kernels for 0%

commit v1 on v0

v1 whole, which is shorter than its diff:
```python
import functools

import jax
import jax.numpy as jnp
import numpy as np
from jax import lax
from jax.experimental import pallas as pl
from jax.experimental.pallas import tpu as pltpu
from jax.sharding import PartitionSpec as P

FIELDS = 4
NLON = 5120
M = 1280
NL = 1280
REACH = 4
LEV = 16
ROWS = 2
TARGETS = ROWS + 2
SECTORS = 8
BANDS = 32
COLS = NLON // SECTORS
WIDE = 768
PER_PEER = LEV // SECTORS
LINES = TARGETS * FIELDS * PER_PEER
SLOTS = M // BANDS
LANE_SLOTS = 8
GROUPS = SLOTS // LANE_SLOTS
MSG = TARGETS * (GROUPS + 1)
NLAT = ROWS * BANDS
VMEM = 56 * 1024 * 1024

F32 = jnp.float32
BF16 = jnp.bfloat16


def dot(a, b, dims):
    return lax.dot_general(a, b, (dims, ((), ())), preferred_element_type=F32)


def level_order():
    order = np.zeros((FIELDS * TARGETS * LEV, FIELDS * TARGETS * LEV), np.float32)
    for peer in range(SECTORS):
        for t in range(TARGETS):
            for f in range(FIELDS):
                for v in range(PER_PEER):
                    out = ((peer * TARGETS + t) * FIELDS + f) * PER_PEER + v
                    order[out, (f * TARGETS + t) * LEV + peer * PER_PEER + v] = 1
    return order.astype(BF16)


def message_order():
    order = np.zeros((BANDS * MSG, TARGETS * BANDS * GROUPS), np.float32)
    for k in range(BANDS):
        for t in range(TARGETS):
            for g in range(GROUPS):
                order[k * MSG + t * (GROUPS + 1) + g, (t * BANDS + k) * GROUPS + g] = 1
    return order.astype(BF16)


def latitude_order():
    order = np.zeros((BANDS * MSG, (GROUPS + 1) * 2 * NLAT), np.float32)
    for k in range(BANDS):
        for t in range(TARGETS):
            i = ROWS * k + t - 1
            if 0 <= i < NLAT:
                for g in range(GROUPS + 1):
                    for twice in range(2):
                        order[k * MSG + t * (GROUPS + 1) + g, (g * 2 + twice) * NLAT + i] = 1
    return order.astype(BF16)


def deposit_kernel(grid_ref, weight_ref, offset_ref, order_ref, out_ref, coef, stacked):
    zeros = jnp.zeros((LEV, COLS), F32)
    for i in range(ROWS):
        offs = offset_ref[i]
        south = offs[:, 0, :] == -1
        east = offs[:, 1, :]
        wide_weights = weight_ref[i].astype(F32)
        w = [wide_weights[:, c, :] for c in range(4)]
        by_row = (
            [jnp.where(south, w[q], zeros) for q in range(2)],
            [jnp.where(south, w[2 + q], w[q]) for q in range(2)],
            [jnp.where(south, zeros, w[2 + q]) for q in range(2)],
        )
        for n, shift in enumerate(range(REACH, -REACH - 1, -1)):
            west_here = east == shift
            east_here = east == shift - 1
            for r in range(3):
                coef[n, i, r] = jnp.where(west_here, by_row[r][0], jnp.where(east_here, by_row[r][1], zeros))
    pad = jnp.zeros((8, WIDE - COLS), F32)
    for f in range(FIELDS):
        for half in range(LEV // 8):
            part = pl.ds(8 * half, 8)
            g = [grid_ref[f, i, part, :] for i in range(ROWS)]
            total = [None] * TARGETS
            for n in range(2 * REACH + 1):
                for t in range(TARGETS):
                    piece = None
                    for i in range(ROWS):
                        r = t - i
                        if 0 <= r < 3:
                            term = g[i] * coef[n, i, r, part, :]
                            piece = term if piece is None else piece + term
                    piece = jnp.concatenate([piece, pad], axis=1)
                    if n == 0:
                        total[t] = piece
                    else:
                        total[t] = pltpu.roll(total[t], 1, 1) + piece
            for t in range(TARGETS):
                stacked[pl.ds((f * TARGETS + t) * LEV + 8 * half, 8), :] = total[t]
    ordered = dot(order_ref[...], stacked[...].astype(BF16), ((1,), (0,)))
    out_ref[...] = ordered.astype(BF16).reshape(out_ref.shape)


def sincos(count):
    turn = count - NLON * jnp.round(count * (1.0 / NLON))
    quarter = jnp.round(turn * (4.0 / NLON))
    x = (turn - (NLON // 4) * quarter) * np.float32(2.0 * np.pi / NLON)
    y = x * x
    s = x * (1.0 + y * (-1.0 / 6 + y * (1.0 / 120 + y * (-1.0 / 5040 + y * (1.0 / 362880)))))
    c = 1.0 + y * (-1.0 / 2 + y * (1.0 / 24 + y * (-1.0 / 720 + y * (1.0 / 40320))))
    odd = jnp.abs(quarter) == 1.0
    cosine = jnp.where(odd, s, c)
    sine = jnp.where(odd, c, s)
    cosine = jnp.where((quarter == 1.0) | (jnp.abs(quarter) == 2.0), -cosine, cosine)
    sine = jnp.where((quarter == -1.0) | (jnp.abs(quarter) == 2.0), -sine, sine)
    return cosine, sine


STEP = 32


def table_kernel(mode_ref, table_ref, turn_ref):
    mode = mode_ref[...].astype(F32)

    def rows(count, scale, first):
        index = lax.broadcasted_iota(jnp.int32, (count, M), 0) * scale + first
        return sincos(index.astype(F32) * mode)

    coarse_c, coarse_s = rows(WIDE // STEP, STEP, 0)
    fine_c, fine_s = rows(STEP, 1, -REACH)
    factor = jnp.where(mode == 0.0, 1.0, 2.0)
    fine_c = fine_c * factor
    fine_s = fine_s * factor
    for a in range(WIDE // STEP):
        c = coarse_c[a : a + 1]
        s = coarse_s[a : a + 1]
        table_ref[a * STEP : (a + 1) * STEP, :M] = (c * fine_c - s * fine_s).astype(BF16)
        table_ref[a * STEP : (a + 1) * STEP, M:] = (-s * fine_c - c * fine_s).astype(BF16)
    turn_c, turn_s = rows(SECTORS, COLS, 0)
    turn_ref[0] = turn_c
    turn_ref[1] = turn_s


BLOCK = 256


def fourier_kernel(points_ref, grid_ref, table_ref, turn_ref, order_ref, out_ref, spectra, lanes):
    data = grid_ref[...].reshape(SECTORS * LINES, WIDE)
    for start in range(0, M, BLOCK):
        part = slice(start, start + BLOCK)
        real = dot(data, table_ref[:, part], ((1,), (0,)))
        imag = dot(data, table_ref[:, M + start : M + start + BLOCK], ((1,), (0,)))
        sum_r = jnp.zeros((LINES, BLOCK), F32)
        sum_i = jnp.zeros((LINES, BLOCK), F32)
        for j in range(SECTORS):
            c = turn_ref[0, j : j + 1, part]
            s = turn_ref[1, j : j + 1, part]
            re = real[j * LINES : (j + 1) * LINES]
            im = imag[j * LINES : (j + 1) * LINES]
            sum_r = sum_r + c * re + s * im
            sum_i = sum_i + c * im - s * re
        for t in range(TARGETS):
            rows = slice(8 * t, 8 * t + 8)
            spectra[t, :, part] = jnp.concatenate([sum_r[rows], sum_i[rows]], axis=0).astype(BF16)
    run = BANDS * GROUPS
    for t in range(TARGETS):
        for b in range(LANE_SLOTS):
            lanes[16 * b : 16 * b + 16, t * run : (t + 1) * run] = spectra[t, :, b * run : (b + 1) * run]
    message = dot(order_ref[...], lanes[...], ((1,), (1,)))
    row = lax.broadcasted_iota(jnp.int32, (MSG, 128), 0)
    lane = lax.broadcasted_iota(jnp.int32, (MSG, 128), 1)
    extra = jnp.zeros((MSG, 128), F32)
    for i in range(ROWS):
        count = (points_ref[i] + 1) // 2
        high = count // 16
        value = jnp.where(lane == 0, high, jnp.where(lane == 1, count - 16 * high, 0))
        extra = extra + jnp.where(row == (i + 1) * (GROUPS + 1) + GROUPS, value, 0).astype(F32)
    for k in range(BANDS):
        out_ref[k] = (message[k * MSG : (k + 1) * MSG] + extra).astype(BF16)


def legendre_kernel(mode_ref, band_ref, msg_ref, legendre_ref, order_ref, out_ref):
    base = band_ref[0] * SLOTS
    received = msg_ref[...].reshape(BANDS * MSG, 128)
    spread = dot(received, order_ref[...], ((0,), (0,)))
    lp = spread[:, GROUPS * 128 :]
    limit = 16.0 * lp[0:1] + lp[1:2]
    lane = lax.broadcasted_iota(jnp.int32, (16, 128), 1)
    first = lane < NLAT
    degree = lax.broadcasted_iota(jnp.int32, (16, NL), 1)
    none = jnp.zeros((16, 128), F32)
    for q in range(SLOTS // 4):
        g, half = divmod(q, 2)
        left = []
        for n in range(4):
            b = 4 * half + n
            mode = mode_ref[base + g * LANE_SLOTS + b]
            keep = mode.astype(F32) < limit
            own = first if n % 2 == 0 else ~first
            value = spread[16 * b : 16 * b + 16, g * 128 : (g + 1) * 128]
            value = jnp.where(keep & own, value, none)
            left.append(jnp.concatenate([value, none] if n < 2 else [none, value], axis=1))
        left = jnp.concatenate(left, axis=0).astype(BF16)
        result = dot(left, legendre_ref[q], ((1,), (0,)))
        for n in range(4):
            slot = 4 * q + n
            mode = mode_ref[base + slot]
            block = jnp.where(degree >= mode, result[16 * n : 16 * n + 16], 0.0)
            for r in range(2):
                for f in range(FIELDS):
                    at = (r * FIELDS + f) * PER_PEER
                    out_ref[slot, r, f] = block[at : at + PER_PEER].astype(BF16)


def params():
    return pltpu.CompilerParams(vmem_limit_bytes=VMEM)


def in_vmem():
    return pl.BlockSpec(memory_space=pltpu.VMEM)


def in_smem():
    return pl.BlockSpec(memory_space=pltpu.SMEM)


def per_device(grid_cot, weights, offsets, lat_points, slot_mode, legendre):
    sent = pl.pallas_call(
        deposit_kernel,
        name="deposit",
        out_shape=jax.ShapeDtypeStruct((SECTORS, LINES, WIDE), BF16),
        in_specs=[in_vmem()] * 4,
        out_specs=in_vmem(),
        scratch_shapes=[
            pltpu.VMEM((2 * REACH + 1, ROWS, 3, LEV, COLS), F32),
            pltpu.VMEM((FIELDS * TARGETS * LEV, WIDE), F32),
        ],
        compiler_params=params(),
        cost_estimate=pl.CostEstimate(flops=20_000_000, bytes_accessed=1_500_000, transcendentals=0),
    )(grid_cot, weights, offsets, jnp.asarray(level_order()))
    column_mode = slot_mode.reshape(M // LANE_SLOTS, LANE_SLOTS).T.reshape(1, M)
    table, turn = pl.pallas_call(
        table_kernel,
        name="table",
        out_shape=(
            jax.ShapeDtypeStruct((WIDE, 2 * M), BF16),
            jax.ShapeDtypeStruct((2, SECTORS, M), F32),
        ),
        in_specs=[in_vmem()],
        out_specs=(in_vmem(), in_vmem()),
        compiler_params=params(),
        cost_estimate=pl.CostEstimate(flops=20_000_000, bytes_accessed=4_000_000, transcendentals=0),
    )(column_mode)
    circles = lax.all_to_all(sent, "lon", split_axis=0, concat_axis=0, tiled=True)
    message = pl.pallas_call(
        fourier_kernel,
        name="fourier",
        out_shape=jax.ShapeDtypeStruct((BANDS, MSG, 128), BF16),
        in_specs=[in_smem()] + [in_vmem()] * 4,
        out_specs=in_vmem(),
        scratch_shapes=[
            pltpu.VMEM((TARGETS, 16, M), BF16),
            pltpu.VMEM((128, TARGETS * BANDS * GROUPS), BF16),
        ],
        compiler_params=params(),
        cost_estimate=pl.CostEstimate(flops=1_000_000_000, bytes_accessed=5_000_000, transcendentals=0),
    )(lat_points, circles, table, turn, jnp.asarray(message_order()))
    coefficients = lax.all_to_all(message, "lat", split_axis=0, concat_axis=0, tiled=True)
    band = lax.axis_index("lat").astype(jnp.int32).reshape(1)
    return pl.pallas_call(
        legendre_kernel,
        name="legendre",
        out_shape=jax.ShapeDtypeStruct((SLOTS, 2, FIELDS, PER_PEER, NL), BF16),
        in_specs=[in_smem(), in_smem()] + [in_vmem()] * 3,
        out_specs=in_vmem(),
        compiler_params=params(),
        cost_estimate=pl.CostEstimate(flops=500_000_000, bytes_accessed=8_000_000, transcendentals=0),
    )(
        slot_mode,
        band,
        coefficients,
        legendre.reshape(SLOTS // 4, 4 * NLAT, NL),
        jnp.asarray(latitude_order()),
    )


def solution(mesh):
    placed = (
        P(None, "lat", None, "lon"),
        P("lat", None, None, "lon"),
        P("lat", None, None, "lon"),
        P("lat"),
        P(),
        P("lat", None, None),
    )
    return jax.shard_map(
        per_device,
        mesh=mesh,
        in_specs=placed,
        out_specs=P("lat", None, None, "lon", None),
        check_vma=False,
    )
```

time: 179 us -> 57.8 us (0.32)
  matrix products: 54 us -> 0 us
  local copies, waits for them, and re-layouts: 43.8 us -> 2.95 us
  other arithmetic: 36.2 us -> 0 us
  Pallas kernels: 0 us -> 21.8 us
  starting transfers between devices: 29.1 us -> 18.4 us
    dot_general x9 -> x0, matrix products: 54 us -> none  [the longest x8 50.1 us: add_sector(): jnp.dot(sector_grid, base_table, precision=lax.Precision.HIGHEST, preferr...]
    pallas_call x0 -> x4, Pallas kernels: none -> 21.8 us  [the longest x1 6.86 us: per_device(): pl.pallas_call(deposit_kernel, name='deposit', out_shape=jax.ShapeDtypeSt...]
    mul x2 -> x0, other arithmetic: 14.4 us -> none  [the longest x1 14.4 us: fourier_table(): -factor * jnp.sin(angle)]
    ppermute x4 -> x0, starting transfers between devices: 10.7 us -> none  [the longest x2 6.53 us: padded(): before = lax.ppermute(last, axis, up)]
    unnamed x6 -> x4, local copies, waits for them, and re-layouts: 11.3 us -> 1.41 us
    gather x1 -> x0, local copies, waits for them, and re-layouts: 9.28 us -> none  [per_device(): ordered = jnp.take(masked, slot_mode, axis=4)]
    add x21 -> x0, other arithmetic: 7.98 us -> none  [the longest x1 3.28 us: deposit_local(): deposit + jnp.pad(piece, ((0, 0), (row_shift + 1, 1 - row_shift), (0, 0),...]
    slice x6 -> x0, local copies, waits for them, and re-layouts: 6.45 us -> none  [the longest x2 1.7 us: padded(): first = lax.slice_in_dim(value, 0, width, axis=dim)]
  transfers between devices with their start and end apart: 6 -> 2, of which waited for: 3 -> 2; matrix products, arithmetic and copies ran while one was open for 14% -> 3% of each run, Pallas kernels for 0% -> 7%
where the time goes in v1:
time: 57.8 us; the launch traced here: 57.4 us
  Pallas kernels  21.8 us (38%)
  starting transfers between devices  18.4 us (32%)
  waiting for transfers between devices  14.2 us (25%)
  local copies, waits for them, and re-layouts  2.95 us (5%)
    all_to_all x1, starting transfers between devices, per_device(): lax.all_to_all(message, 'lat', split_axis=0, concat_axis=0, tiled=True)  12.2 us
    all_to_all x1, waiting for transfers between devices, per_device(): lax.all_to_all(message, 'lat', split_axis=0, concat_axis=0, tiled=True)  12 us
    pallas_call x1, Pallas kernels, per_device(): pl.pallas_call(deposit_kernel, name='deposit', out_shape=jax.ShapeDtypeSt...  6.86 us
    all_to_all x1, starting transfers between devices, per_device(): lax.all_to_all(sent, 'lon', split_axis=0, concat_axis=0, tiled=True)  6.2 us
    pallas_call x1, Pallas kernels, per_device(): pl.pallas_call(legendre_kernel, name='legendre', out_shape=jax.ShapeDtype...  6.07 us
    pallas_call x1, Pallas kernels, per_device(): pl.pallas_call(fourier_kernel, name='fourier', out_shape=jax.ShapeDtypeSt...  4.9 us
    pallas_call x1, Pallas kernels, per_device(): pl.pallas_call(table_kernel, name='table', out_shape=(jax.ShapeDtypeStruc...  4.01 us
    all_to_all x1, waiting for transfers between devices, per_device(): lax.all_to_all(sent, 'lon', split_axis=0, concat_axis=0, tiled=True)  2.23 us
  transfers between devices with their start and end apart: 2, of which 2 were waited for; matrix products, arithmetic and copies ran while one was open for 3% of the time, Pallas kernels for 7%

profile of v1, /device:TPU:1, one launch (start us, length us, event | category | flops | bytes accessed | tf_op | source)
XLA Modules:
  0.0 57.4 jit_solution(3236542323288394230)
XLA Ops:
  0.0 6.9 %deposit.1 = bf16[8,32,768]{2,1,0:T(8,128)(2,1)} custom-call(f32[4,2,16,640]{3,2,1,0:T(8,128)} %grid_ref.1, bf16[2,16,4,640]{3,2,1,0:T(4,128)(2,1)} %weight_ref.1, s32[2,16,2,640]{3,2,1,0:T(2,128)} %offset_ref.1, bf16[256,256]{1,0:T(8,128)(2,1)} %constant.12.clone.order_ref), custom_call_target="tpu_custom_call" | custom-call | flops 20000000 | bytes 1500000 | tf_op jit(solution)/shard_map/deposit/pallas_call | solution.py:239
  6.9 6.2 %all-to-all-start = ((bf16[8,32,768]{2,1,0:T(8,128)(2,1)}), bf16[8,32,768]{2,1,0:T(8,128)(2,1)S(1)}, u32[]{:S(2)}, u32[]{:S(2)}) async-start(bf16[8,32,768]{2,1,0:T(8,128)(2,1)} %deposit.1), calls=%async_computation | async-start | bytes 786432 | tf_op jit(solution)/shard_map/all_to_all | solution.py:265
  13.1 0.8 %reshape.13 = s32[160,8]{1,0:T(8,128)S(1)} reshape(s32[1280]{0:T(1024)} %mode_ref.1) | data formatting | bytes 10240 | tf_op jit(solution)/shard_map/reshape | solution.py:252
  13.9 0.1 copy.10
  13.9 0.7 %reshape.14.mode_ref = s32[1,1280]{1,0:T(1,128)} reshape(s32[8,160]{1,0:T(8,128)S(1)} %copy.10) | data formatting | bytes 10240 | tf_op jit(solution)/shard_map/reshape | solution.py:252
  14.6 4.0 %table.1 = (bf16[768,2560]{1,0:T(8,128)(2,1)}, f32[2,8,1280]{2,1,0:T(8,128)}) custom-call(s32[1,1280]{1,0:T(1,128)} %reshape.14.mode_ref), custom_call_target="tpu_custom_call" | custom-call | flops 20000000 | bytes 4000000 | tf_op jit(solution)/shard_map/table/pallas_call | solution.py:253
  18.6 2.2 %all-to-all-done.grid_ref = bf16[8,32,768]{2,1,0:T(8,128)(2,1)S(1)} async-done(((bf16[8,32,768]{2,1,0:T(8,128)(2,1)}), bf16[8,32,768]{2,1,0:T(8,128)(2,1)S(1)}, u32[]{:S(2)}, u32[]{:S(2)}) %all-to-all-start) | async-done | bytes 393248 | tf_op jit(solution)/shard_map/all_to_all | solution.py:265
  20.8 0.0 copy-start
  20.8 0.7 %copy-done = bf16[8,32,768]{2,1,0:T(8,128)(2,1)} copy-done((bf16[8,32,768]{2,1,0:T(8,128)(2,1)}, bf16[8,32,768]{2,1,0:T(8,128)(2,1)S(1)}, u32[]{:S(2)}) %copy-start) | copy-done | bytes 393240
  21.6 4.9 %fourier.1 = bf16[32,24,128]{2,1,0:T(8,128)(2,1)} custom-call(s32[2]{0:T(128)} %points_ref.1, bf16[8,32,768]{2,1,0:T(8,128)(2,1)} %copy-done, bf16[768,2560]{1,0:T(8,128)(2,1)} %get-tuple-element.7.table_ref, f32[2,8,1280]{2,1,0:T(8,128)} %get-tuple-element.8.turn_ref, bf16[768,640]{1,0:T(8,128)(2,1)} %constant.13.clone.order_ref), custom_call_target="tpu_custom_call" | custom-call | flops 1000000000 | bytes 5000000 | tf_op jit(solution)/shard_map/fourier/pallas_call | solution.py:266
  26.5 12.2 %all-to-all-start.1 = ((bf16[32,24,128]{2,1,0:T(8,128)(2,1)}), bf16[32,24,128]{2,1,0:T(8,128)(2,1)S(1)}, u32[]{:S(2)}, u32[]{:S(2)}) async-start(bf16[32,24,128]{2,1,0:T(8,128)(2,1)} %fourier.1), calls=%async_computation.1 | async-start | bytes 393216 | tf_op jit(solution)/shard_map/all_to_all | solution.py:279
  38.7 12.0 %all-to-all-done.1.msg_ref = bf16[32,24,128]{2,1,0:T(8,128)(2,1)S(1)} async-done(((bf16[32,24,128]{2,1,0:T(8,128)(2,1)}), bf16[32,24,128]{2,1,0:T(8,128)(2,1)S(1)}, u32[]{:S(2)}, u32[]{:S(2)}) %all-to-all-start.1) | async-done | bytes 196640 | tf_op jit(solution)/shard_map/all_to_all | solution.py:279
  50.7 0.0 copy-start.1
  50.7 0.7 %copy-done.1 = bf16[32,24,128]{2,1,0:T(8,128)(2,1)} copy-done((bf16[32,24,128]{2,1,0:T(8,128)(2,1)}, bf16[32,24,128]{2,1,0:T(8,128)(2,1)S(1)}, u32[]{:S(2)}) %copy-start.1) | copy-done | bytes 196632
  51.4 6.1 %legendre.1 = bf16[40,2,4,2,1280]{4,3,2,1,0:T(2,128)(2,1)} custom-call(s32[1280]{0:T(1024)} %mode_ref.1, s32[1]{0:T(128)} %bitcast.band_ref, bf16[32,24,128]{2,1,0:T(8,128)(2,1)} %copy-done.1, bf16[10,256,1280]{2,1,0:T(8,128)(2,1)} %bitcast.3, bf16[768,768]{1,0:T(8,128)(2,1)} %constant.14.clone.order_ref), custom_call_target="tpu_custom_call" | custom-call | flops 500000000 | bytes 8000000 | tf_op jit(solution)/shard_map/legendre/pallas_call | solution.py:281
Async XLA Ops:
  6.9 14.0 %all-to-all-start = ((bf16[8,32,768]{2,1,0:T(8,128)(2,1)}), bf16[8,32,768]{2,1,0:T(8,128)(2,1)S(1)}, u32[]{:S(2)}, u32[]{:S(2)}) async-start(bf16[8,32,768]{2,1,0:T(8,128)(2,1)} %deposit.1), calls=%async_computation | async-start | bytes 786432 | tf_op jit(solution)/shard_map/all_to_all | solution.py:265
  20.8 0.7 %copy-start = (bf16[8,32,768]{2,1,0:T(8,128)(2,1)}, bf16[8,32,768]{2,1,0:T(8,128)(2,1)S(1)}, u32[]{:S(2)}) copy-start(bf16[8,32,768]{2,1,0:T(8,128)(2,1)S(1)} %all-to-all-done.grid_ref) | copy-start | bytes 1179652
  26.5 24.2 %all-to-all-start.1 = ((bf16[32,24,128]{2,1,0:T(8,128)(2,1)}), bf16[32,24,128]{2,1,0:T(8,128)(2,1)S(1)}, u32[]{:S(2)}, u32[]{:S(2)}) async-start(bf16[32,24,128]{2,1,0:T(8,128)(2,1)} %fourier.1), calls=%async_computation.1 | async-start | bytes 393216 | tf_op jit(solution)/shard_map/all_to_all | solution.py:279
  50.7 0.7 %copy-start.1 = (bf16[32,24,128]{2,1,0:T(8,128)(2,1)}, bf16[32,24,128]{2,1,0:T(8,128)(2,1)S(1)}, u32[]{:S(2)}) copy-start(bf16[32,24,128]{2,1,0:T(8,128)(2,1)S(1)} %all-to-all-done.1.msg_ref) | copy-start | bytes 589828

commit v2 on v1

v2 whole, which is shorter than its diff:
```python
import functools

import jax
import jax.numpy as jnp
import numpy as np
from jax import lax
from jax.experimental import pallas as pl
from jax.experimental.pallas import tpu as pltpu
from jax.sharding import PartitionSpec as P

FIELDS = 4
NLON = 5120
M = 1280
NL = 1280
REACH = 4
LEV = 16
ROWS = 2
TARGETS = ROWS + 2
SECTORS = 8
BANDS = 32
COLS = NLON // SECTORS
WIDE = 768
PER_PEER = LEV // SECTORS
LINES = TARGETS * FIELDS * PER_PEER
SLOTS = M // BANDS
LANE_SLOTS = 8
GROUPS = SLOTS // LANE_SLOTS
MSG = TARGETS * (GROUPS + 1)
NLAT = ROWS * BANDS

F32 = jnp.float32
BF16 = jnp.bfloat16


def dot(a, b, dims):
    return lax.dot_general(a, b, (dims, ((), ())), preferred_element_type=F32)


def spread_order():
    order = np.zeros((6 * ROWS * LEV, 6 * FIELDS * ROWS * LEV), np.float32)
    for c in range(6):
        for f in range(FIELDS):
            for n in range(ROWS * LEV):
                row = n * 4 + c if c < 4 else ROWS * LEV * 4 + n * 2 + c - 4
                order[row, (c * FIELDS + f) * ROWS * LEV + n] = 1
    return order.astype(BF16)


def level_order():
    order = np.zeros((SECTORS * LINES, 3, 2, FIELDS, ROWS, LEV), np.float32)
    for peer in range(SECTORS):
        for t in range(TARGETS):
            for f in range(FIELDS):
                for v in range(PER_PEER):
                    out = ((peer * TARGETS + t) * FIELDS + f) * PER_PEER + v
                    for i in range(ROWS):
                        if 0 <= t - i < 3:
                            order[out, t - i, :, f, i, peer * PER_PEER + v] = 1
    return order.reshape(SECTORS * LINES, -1).astype(BF16)


def message_order():
    order = np.zeros((BANDS * MSG, TARGETS * BANDS * GROUPS), np.float32)
    for k in range(BANDS):
        for t in range(TARGETS):
            for g in range(GROUPS):
                order[k * MSG + t * (GROUPS + 1) + g, (t * BANDS + k) * GROUPS + g] = 1
    return order.astype(BF16)


def latitude_order():
    order = np.zeros((BANDS * MSG, (GROUPS + 1) * 2 * NLAT), np.float32)
    for k in range(BANDS):
        for t in range(TARGETS):
            i = ROWS * k + t - 1
            if 0 <= i < NLAT:
                for g in range(GROUPS + 1):
                    for twice in range(2):
                        order[k * MSG + t * (GROUPS + 1) + g, (g * 2 + twice) * NLAT + i] = 1
    return order.astype(BF16)


LANES = FIELDS * ROWS * LEV


def deposit_kernel(
    grid_hbm, weight_hbm, offset_hbm, spread_hbm, order_hbm, out_ref,
    grid, weight, offset, spread, order, sems, stacked, wide, terms, parts,
):
    pairs = (
        (offset_hbm, offset), (weight_hbm, weight), (spread_hbm, spread), (grid_hbm, grid), (order_hbm, order),
    )
    copies = [pltpu.make_async_copy(src, dst, sems.at[n]) for n, (src, dst) in enumerate(pairs)]
    for copy in copies:
        copy.start()
    for n in range(7):
        fill = jnp.full((8, LANES), 99.0 if n == 0 else 0.0, F32)
        terms[n, 0:8] = fill
        terms[n, COLS + 8 : COLS + 16] = fill
    copies[0].wait()
    for i in range(ROWS):
        for v in range(LEV):
            at = ROWS * LEV * 4 + (i * LEV + v) * 2
            stacked[at : at + 2, :] = offset[i, v].astype(F32)
    copies[1].wait()
    for i in range(ROWS):
        for v in range(LEV):
            at = (i * LEV + v) * 4
            stacked[at : at + 4, :] = weight[i, v].astype(F32)
    copies[2].wait()
    wide[...] = dot(stacked[...].astype(BF16), spread[...], ((0,), (0,)))
    copies[3].wait()
    for j in range(COLS // 128):
        rows = slice(128 * j, 128 * j + 128)
        lines = slice(128 * j + 8, 128 * j + 136)
        g = grid[:, :, :, rows].reshape(LANES, 128).T
        w = [g * wide[rows, c * LANES : (c + 1) * LANES] for c in range(4)]
        south = wide[rows, 4 * LANES : 5 * LANES] < -0.5
        terms[0, lines] = wide[rows, 5 * LANES :]
        for q in range(2):
            terms[1 + q, lines] = jnp.where(south, w[q], 0.0)
            terms[3 + q, lines] = jnp.where(south, w[2 + q], w[q])
            terms[5 + q, lines] = jnp.where(south, 0.0, w[2 + q])

    def tile(start):
        total = [jnp.zeros((8, LANES), F32) for _ in range(3)]
        for n in range(2 * REACH + 1):
            shift = REACH - n
            east = terms[0, pl.ds(start + n, 8), :]
            here = east == float(shift)
            before = east == float(shift - 1)
            for r in range(3):
                first = terms[1 + 2 * r, pl.ds(start + n, 8), :]
                second = terms[2 + 2 * r, pl.ds(start + n, 8), :]
                total[r] = total[r] + jnp.where(here, first, jnp.where(before, second, 0.0))
        return total

    def step(n, carry):
        start = pl.multiple_of(n * 16, 16)
        top = tile(start)
        bottom = tile(start + 8)
        for r in range(3):
            whole = jnp.concatenate([top[r], bottom[r]], axis=0)
            high = whole.astype(BF16)
            low = (whole - high.astype(F32)).astype(BF16)
            parts[pl.ds(start, 16), 2 * r * LANES : (2 * r + 1) * LANES] = high
            parts[pl.ds(start, 16), (2 * r + 1) * LANES : (2 * r + 2) * LANES] = low
        return carry

    lax.fori_loop(0, COLS // 16, step, 0)
    edge = tile(COLS)
    parts[COLS:, :] = jnp.zeros((WIDE - COLS, 6 * LANES), BF16)
    for r in range(3):
        whole = jnp.concatenate([edge[r], jnp.zeros((8, LANES), F32)], axis=0)
        high = whole.astype(BF16)
        low = (whole - high.astype(F32)).astype(BF16)
        parts[COLS : COLS + 16, 2 * r * LANES : (2 * r + 1) * LANES] = high
        parts[COLS : COLS + 16, (2 * r + 1) * LANES : (2 * r + 2) * LANES] = low
    copies[4].wait()
    ordered = dot(order[...], parts[...], ((1,), (1,)))
    out_ref[...] = ordered.astype(BF16).reshape(out_ref.shape)


def sincos(count):
    turn = count - NLON * jnp.round(count * (1.0 / NLON))
    quarter = jnp.round(turn * (4.0 / NLON))
    x = (turn - (NLON // 4) * quarter) * np.float32(2.0 * np.pi / NLON)
    y = x * x
    s = x * (1.0 + y * (-1.0 / 6 + y * (1.0 / 120 + y * (-1.0 / 5040 + y * (1.0 / 362880)))))
    c = 1.0 + y * (-1.0 / 2 + y * (1.0 / 24 + y * (-1.0 / 720 + y * (1.0 / 40320))))
    odd = jnp.abs(quarter) == 1.0
    cosine = jnp.where(odd, s, c)
    sine = jnp.where(odd, c, s)
    cosine = jnp.where((quarter == 1.0) | (jnp.abs(quarter) == 2.0), -cosine, cosine)
    sine = jnp.where((quarter == -1.0) | (jnp.abs(quarter) == 2.0), -sine, sine)
    return cosine, sine


STEP = 32
BLOCK = 256
BLOCKS = M // BLOCK
AUX = 24


def table_kernel(points_ref, mode_ref, table_hbm, aux_hbm, table, aux, sems):
    mode = mode_ref[...].astype(F32)

    def rows(count, scale, first):
        index = lax.broadcasted_iota(jnp.int32, (count, M), 0) * scale + first
        return sincos(index.astype(F32) * mode)

    coarse_c, coarse_s = rows(WIDE // STEP, STEP, 0)
    fine_c, fine_s = rows(STEP, 1, -REACH)
    factor = jnp.where(mode == 0.0, 1.0, 2.0)
    fine_c = fine_c * factor
    fine_s = fine_s * factor
    copies = []
    for n in range(BLOCKS):
        part = slice(n * BLOCK, (n + 1) * BLOCK)
        for a in range(WIDE // STEP):
            c = coarse_c[a : a + 1, part]
            s = coarse_s[a : a + 1, part]
            lines = slice(a * STEP, (a + 1) * STEP)
            table[n, lines, :BLOCK] = (c * fine_c[:, part] - s * fine_s[:, part]).astype(BF16)
            table[n, lines, BLOCK:] = (-s * fine_c[:, part] - c * fine_s[:, part]).astype(BF16)
        copies.append(pltpu.make_async_copy(table.at[n], table_hbm.at[n], sems.at[n]))
        copies[-1].start()
    turn_c, turn_s = rows(SECTORS, COLS, 0)
    aux[0:SECTORS, :] = turn_c
    aux[SECTORS : 2 * SECTORS, :] = turn_s
    row = lax.broadcasted_iota(jnp.int32, (AUX - 2 * SECTORS, M), 0)
    lane = lax.broadcasted_iota(jnp.int32, (AUX - 2 * SECTORS, M), 1)
    extra = jnp.zeros((AUX - 2 * SECTORS, M), F32)
    for i in range(ROWS):
        count = (points_ref[i] + 1) // 2
        high = count // 16
        value = jnp.where(lane == 0, high, jnp.where(lane == 1, count - 16 * high, 0))
        extra = extra + jnp.where(row == i, value, 0).astype(F32)
    aux[2 * SECTORS :, :] = extra
    copies.append(pltpu.make_async_copy(aux, aux_hbm, sems.at[BLOCKS]))
    copies[-1].start()
    for copy in copies:
        copy.wait()


def fourier_kernel(grid_ref, table_hbm, aux_hbm, order_hbm, out_ref, table, aux, order, sems, spectra, lanes):
    copies = [pltpu.make_async_copy(aux_hbm, aux, sems.at[BLOCKS])]
    copies += [pltpu.make_async_copy(table_hbm.at[n], table.at[n], sems.at[n]) for n in range(BLOCKS)]
    copies.append(pltpu.make_async_copy(order_hbm, order, sems.at[BLOCKS + 1]))
    for copy in copies:
        copy.start()
    copies[0].wait()
    data = grid_ref[...].reshape(SECTORS * LINES, WIDE)
    for n in range(BLOCKS):
        part = slice(n * BLOCK, (n + 1) * BLOCK)
        copies[1 + n].wait()
        real = dot(data, table[n, :, :BLOCK], ((1,), (0,)))
        imag = dot(data, table[n, :, BLOCK:], ((1,), (0,)))
        sum_r = jnp.zeros((LINES, BLOCK), F32)
        sum_i = jnp.zeros((LINES, BLOCK), F32)
        for j in range(SECTORS):
            c = aux[j : j + 1, part]
            s = aux[SECTORS + j : SECTORS + j + 1, part]
            re = real[j * LINES : (j + 1) * LINES]
            im = imag[j * LINES : (j + 1) * LINES]
            sum_r = sum_r + c * re + s * im
            sum_i = sum_i + c * im - s * re
        for t in range(TARGETS):
            rows = slice(8 * t, 8 * t + 8)
            spectra[t, :, part] = jnp.concatenate([sum_r[rows], sum_i[rows]], axis=0).astype(BF16)
    run = BANDS * GROUPS
    for t in range(TARGETS):
        for b in range(LANE_SLOTS):
            lanes[16 * b : 16 * b + 16, t * run : (t + 1) * run] = spectra[t, :, b * run : (b + 1) * run]
    copies[-1].wait()
    message = dot(order[...], lanes[...], ((1,), (1,)))
    row = lax.broadcasted_iota(jnp.int32, (MSG, 128), 0)
    extra = jnp.zeros((MSG, 128), F32)
    for i in range(ROWS):
        limit = aux[2 * SECTORS + i : 2 * SECTORS + i + 1, 0:128]
        extra = jnp.where(row == (i + 1) * (GROUPS + 1) + GROUPS, limit, extra)
    for k in range(BANDS):
        out_ref[k] = (message[k * MSG : (k + 1) * MSG] + extra).astype(BF16)


def legendre_kernel(mode_ref, msg_ref, legendre_hbm, order_hbm, out_hbm, legendre, order, out, sems):
    quads = SLOTS // 4
    copies = [pltpu.make_async_copy(order_hbm, order, sems.at[quads])]
    copies += [pltpu.make_async_copy(legendre_hbm.at[q], legendre.at[q], sems.at[q]) for q in range(quads)]
    for copy in copies:
        copy.start()
    base = lax.axis_index("lat") * SLOTS
    received = msg_ref[...].reshape(BANDS * MSG, 128)
    copies[0].wait()
    spread = dot(received, order[...], ((0,), (0,)))
    lp = spread[:, GROUPS * 128 :]
    limit = 16.0 * lp[0:1] + lp[1:2]
    lane = lax.broadcasted_iota(jnp.int32, (16, 128), 1)
    first = lane < NLAT
    degree = lax.broadcasted_iota(jnp.int32, (16, NL), 1)
    none = jnp.zeros((16, 128), F32)
    sent = []
    for q in range(quads):
        g, half = divmod(q, 2)
        left = []
        for n in range(4):
            b = 4 * half + n
            mode = mode_ref[base + g * LANE_SLOTS + b]
            keep = mode.astype(F32) < limit
            own = first if n % 2 == 0 else ~first
            value = spread[16 * b : 16 * b + 16, g * 128 : (g + 1) * 128]
            value = jnp.where(keep & own, value, none)
            left.append(jnp.concatenate([value, none] if n < 2 else [none, value], axis=1))
        left = jnp.concatenate(left, axis=0).astype(BF16)
        copies[1 + q].wait()
        result = dot(left, legendre[q], ((1,), (0,)))
        for n in range(4):
            slot = 4 * q + n
            mode = mode_ref[base + slot]
            block = jnp.where(degree >= mode, result[16 * n : 16 * n + 16], 0.0)
            for r in range(2):
                for f in range(FIELDS):
                    at = (r * FIELDS + f) * PER_PEER
                    out[slot, r, f] = block[at : at + PER_PEER].astype(BF16)
        here = pl.ds(4 * q, 4)
        sent.append(pltpu.make_async_copy(out.at[here], out_hbm.at[here], sems.at[quads + 1 + q]))
        sent[-1].start()
    for copy in sent:
        copy.wait()


def params(mib):
    return pltpu.CompilerParams(vmem_limit_bytes=mib * 1024 * 1024)


def in_vmem():
    return pl.BlockSpec(memory_space=pltpu.VMEM)


def in_hbm():
    return pl.BlockSpec(memory_space=pltpu.HBM)


def in_smem():
    return pl.BlockSpec(memory_space=pltpu.SMEM)


def per_device(grid_cot, weights, offsets, lat_points, slot_mode, legendre):
    sent = pl.pallas_call(
        deposit_kernel,
        name="deposit",
        out_shape=jax.ShapeDtypeStruct((SECTORS, LINES, WIDE), BF16),
        in_specs=[in_hbm()] * 5,
        out_specs=in_vmem(),
        scratch_shapes=[
            pltpu.VMEM(grid_cot.shape, F32),
            pltpu.VMEM(weights.shape, BF16),
            pltpu.VMEM(offsets.shape, jnp.int32),
            pltpu.VMEM((6 * ROWS * LEV, 6 * LANES), BF16),
            pltpu.VMEM((SECTORS * LINES, 6 * LANES), BF16),
            pltpu.SemaphoreType.DMA((5,)),
            pltpu.VMEM((6 * ROWS * LEV, COLS), F32),
            pltpu.VMEM((COLS, 6 * LANES), F32),
            pltpu.VMEM((7, COLS + 16, LANES), F32),
            pltpu.VMEM((WIDE, 6 * LANES), BF16),
        ],
        compiler_params=params(14),
        cost_estimate=pl.CostEstimate(flops=20_000_000, bytes_accessed=1_500_000, transcendentals=0),
    )(grid_cot, weights, offsets, jnp.asarray(spread_order()), jnp.asarray(level_order()))
    column_mode = slot_mode.reshape(M // LANE_SLOTS, LANE_SLOTS).T.reshape(1, M)
    table, aux = pl.pallas_call(
        table_kernel,
        name="table",
        out_shape=(
            jax.ShapeDtypeStruct((BLOCKS, WIDE, 2 * BLOCK), BF16),
            jax.ShapeDtypeStruct((AUX, M), F32),
        ),
        in_specs=[in_smem(), in_vmem()],
        out_specs=(in_hbm(), in_hbm()),
        scratch_shapes=[
            pltpu.VMEM((BLOCKS, WIDE, 2 * BLOCK), BF16),
            pltpu.VMEM((AUX, M), F32),
            pltpu.SemaphoreType.DMA((BLOCKS + 1,)),
        ],
        compiler_params=params(12),
        cost_estimate=pl.CostEstimate(flops=20_000_000, bytes_accessed=4_000_000, transcendentals=0),
    )(lat_points, column_mode)
    circles = lax.all_to_all(sent, "lon", split_axis=0, concat_axis=0, tiled=True)
    message = pl.pallas_call(
        fourier_kernel,
        name="fourier",
        out_shape=jax.ShapeDtypeStruct((BANDS, MSG, 128), BF16),
        in_specs=[in_vmem()] + [in_hbm()] * 3,
        out_specs=in_vmem(),
        scratch_shapes=[
            pltpu.VMEM((BLOCKS, WIDE, 2 * BLOCK), BF16),
            pltpu.VMEM((AUX, M), F32),
            pltpu.VMEM((BANDS * MSG, TARGETS * BANDS * GROUPS), BF16),
            pltpu.SemaphoreType.DMA((BLOCKS + 2,)),
            pltpu.VMEM((TARGETS, 16, M), BF16),
            pltpu.VMEM((128, TARGETS * BANDS * GROUPS), BF16),
        ],
        compiler_params=params(14),
        cost_estimate=pl.CostEstimate(flops=1_000_000_000, bytes_accessed=5_000_000, transcendentals=0),
    )(circles, table, aux, jnp.asarray(message_order()))
    coefficients = lax.all_to_all(message, "lat", split_axis=0, concat_axis=0, tiled=True)
    shape = (SLOTS, 2, FIELDS, PER_PEER, NL)
    quads = SLOTS // 4
    return pl.pallas_call(
        legendre_kernel,
        name="legendre",
        out_shape=jax.ShapeDtypeStruct(shape, BF16),
        in_specs=[in_smem(), in_vmem()] + [in_hbm()] * 2,
        out_specs=in_hbm(),
        scratch_shapes=[
            pltpu.VMEM((quads, 4 * NLAT, NL), BF16),
            pltpu.VMEM((BANDS * MSG, (GROUPS + 1) * 2 * NLAT), BF16),
            pltpu.VMEM(shape, BF16),
            pltpu.SemaphoreType.DMA((2 * quads + 1,)),
        ],
        compiler_params=params(20),
        cost_estimate=pl.CostEstimate(flops=500_000_000, bytes_accessed=8_000_000, transcendentals=0),
    )(slot_mode, coefficients, legendre.reshape(quads, 4 * NLAT, NL), jnp.asarray(latitude_order()))


def solution(mesh):
    placed = (
        P(None, "lat", None, "lon"),
        P("lat", None, None, "lon"),
        P("lat", None, None, "lon"),
        P("lat"),
        P(),
        P("lat", None, None),
    )
    return jax.shard_map(
        per_device,
        mesh=mesh,
        in_specs=placed,
        out_specs=P("lat", None, None, "lon", None),
        check_vma=False,
    )
```

time: 57.8 us -> 64.4 us (1.11)
  blocking collectives: 0 us -> 24 us
  waiting for transfers between devices: 14.2 us -> 1.68 us
  starting transfers between devices: 18.4 us -> 6.21 us
  local copies, waits for them, and re-layouts: 2.95 us -> 14.4 us
  Pallas kernels: 21.8 us -> 17.5 us
    all_to_all x0 -> x1, blocking collectives: none -> 24 us  [per_device(): lax.all_to_all(message, 'lat', split_axis=0, concat_axis=0, tiled=True)]
    all_to_all x1 -> x0, starting transfers between devices: 12.2 us -> none  [per_device(): lax.all_to_all(message, 'lat', split_axis=0, concat_axis=0, tiled=True)]
    unnamed x4 -> x24, local copies, waits for them, and re-layouts: 1.41 us -> 13.4 us
    all_to_all x1 -> x0, waiting for transfers between devices: 12 us -> none  [per_device(): lax.all_to_all(message, 'lat', split_axis=0, concat_axis=0, tiled=True)]
    pallas_call x1, Pallas kernels: 6.86 us -> 4.94 us  [per_device(): pl.pallas_call(deposit_kernel, name='deposit', out_shape=jax.ShapeDtypeSt...]
    pallas_call x1, Pallas kernels: 4.9 us -> 3.18 us  [per_device(): pl.pallas_call(fourier_kernel, name='fourier', out_shape=jax.ShapeDtypeSt...]
    pallas_call x1, Pallas kernels: 4.01 us -> 2.64 us  [per_device(): pl.pallas_call(table_kernel, name='table', out_shape=(jax.ShapeDtypeStruc...]
    pallas_call x1, Pallas kernels: 6.07 us -> 6.78 us  [per_device(): pl.pallas_call(legendre_kernel, name='legendre', out_shape=jax.ShapeDtype...]
  transfers between devices with their start and end apart: 2 -> 1, of which waited for: 2 -> 1; matrix products, arithmetic and copies ran while one was open for 3% -> 1% of each run, Pallas kernels for 7% -> 4%
where the time goes in v2:
time: 64.4 us; the launch traced here: 63.9 us
  blocking collectives  24 us (37%)
  Pallas kernels  17.5 us (27%)
  local copies, waits for them, and re-layouts  14.4 us (22%)
  starting transfers between devices  6.21 us (10%)
  waiting for transfers between devices  1.68 us (3%)
    all_to_all x1, blocking collectives, per_device(): lax.all_to_all(message, 'lat', split_axis=0, concat_axis=0, tiled=True)  24 us
    unnamed x24, local copies, waits for them, and re-layouts  13.4 us
    pallas_call x1, Pallas kernels, per_device(): pl.pallas_call(legendre_kernel, name='legendre', out_shape=jax.ShapeDtype...  6.78 us
    all_to_all x1, starting transfers between devices, per_device(): lax.all_to_all(sent, 'lon', split_axis=0, concat_axis=0, tiled=True)  6.21 us
    pallas_call x1, Pallas kernels, per_device(): pl.pallas_call(deposit_kernel, name='deposit', out_shape=jax.ShapeDtypeSt...  4.94 us
    pallas_call x1, Pallas kernels, per_device(): pl.pallas_call(fourier_kernel, name='fourier', out_shape=jax.ShapeDtypeSt...  3.18 us
    pallas_call x1, Pallas kernels, per_device(): pl.pallas_call(table_kernel, name='table', out_shape=(jax.ShapeDtypeStruc...  2.64 us
    all_to_all x1, waiting for transfers between devices, per_device(): lax.all_to_all(sent, 'lon', split_axis=0, concat_axis=0, tiled=True)  1.68 us
  transfers between devices with their start and end apart: 1, of which 1 were waited for; matrix products, arithmetic and copies ran while one was open for 1% of the time, Pallas kernels for 4%

profile of v2, /device:TPU:1, one launch (start us, length us, event | category | flops | bytes accessed | tf_op | source)
XLA Modules:
  0.0 63.9 jit_solution(9804549608952083097)
XLA Ops:
  0.0 0.0 copy-start.5
  0.0 1.0 %copy-done.5 = bf16[256,768]{1,0:T(8,128)(2,1)S(1)} copy-done((bf16[256,768]{1,0:T(8,128)(2,1)S(1)}, bf16[256,768]{1,0:T(8,128)(2,1)}, u32[]{:S(2)}) %copy-start.5) | copy-done | bytes 393240
  1.0 0.0 copy-start.6
  1.0 1.0 %copy-done.6 = f32[4,2,16,640]{3,2,1,0:T(8,128)S(1)} copy-done((f32[4,2,16,640]{3,2,1,0:T(8,128)S(1)}, f32[4,2,16,640]{3,2,1,0:T(8,128)}, u32[]{:S(2)}) %copy-start.6) | copy-done | bytes 327704
  2.0 0.0 copy-start.7
  2.0 1.0 %copy-done.7 = bf16[192,768]{1,0:T(8,128)(2,1)S(1)} copy-done((bf16[192,768]{1,0:T(8,128)(2,1)S(1)}, bf16[192,768]{1,0:T(8,128)(2,1)}, u32[]{:S(2)}) %copy-start.7) | copy-done | bytes 294936
  2.9 0.0 copy-start.8
  2.9 0.9 %copy-done.8 = bf16[2,16,4,640]{3,2,1,0:T(4,128)(2,1)S(1)} copy-done((bf16[2,16,4,640]{3,2,1,0:T(4,128)(2,1)S(1)}, bf16[2,16,4,640]{3,2,1,0:T(4,128)(2,1)}, u32[]{:S(2)}) %copy-start.8) | copy-done | bytes 163864
  3.8 0.0 copy-start.9
  3.9 0.9 %copy-done.9 = s32[2,16,2,640]{3,2,1,0:T(2,128)S(1)} copy-done((s32[2,16,2,640]{3,2,1,0:T(2,128)S(1)}, s32[2,16,2,640]{3,2,1,0:T(2,128)}, u32[]{:S(2)}) %copy-start.9) | copy-done | bytes 163864
  4.8 0.0 copy-start.3
  4.8 4.9 %deposit.1 = bf16[8,32,768]{2,1,0:T(8,128)(2,1)} custom-call(f32[4,2,16,640]{3,2,1,0:T(8,128)S(1)} %copy-done.6, bf16[2,16,4,640]{3,2,1,0:T(4,128)(2,1)S(1)} %copy-done.8, s32[2,16,2,640]{3,2,1,0:T(2,128)S(1)} %copy-done.9, bf16[192,768]{1,0:T(8,128)(2,1)S(1)} %copy-done.7, bf16[256,768]{1,0:T(8,128)(2,1)S(1)} %copy-done.5), custom_call_target="tpu_custom_call" | custom-call | flops 20000000 | bytes 1500000 | tf_op jit(solution)/shard_map/deposit/pallas_call | solution.py:329
  9.7 0.0 copy-start.10
  9.7 6.2 %all-to-all-start = ((bf16[8,32,768]{2,1,0:T(8,128)(2,1)}), bf16[8,32,768]{2,1,0:T(8,128)(2,1)S(1)}, u32[]{:S(2)}, u32[]{:S(2)}) async-start(bf16[8,32,768]{2,1,0:T(8,128)(2,1)} %deposit.1), calls=%async_computation | async-start | bytes 786432 | tf_op jit(solution)/shard_map/all_to_all | solution.py:368
  15.9 0.8 %reshape.9 = s32[160,8]{1,0:T(8,128)S(1)} reshape(s32[1280]{0:T(1024)} %mode_ref.1) | data formatting | bytes 10240 | tf_op jit(solution)/shard_map/reshape | solution.py:350
  16.7 0.1 copy.11
  16.8 0.1 reshape.10.mode_ref
  16.9 0.0 copy-start.11
  16.9 0.7 %copy-done.11 = s32[2]{0:T(128)S(1)} copy-done((s32[2]{0:T(128)S(1)}, s32[2]{0:T(128)}, u32[]{:S(2)}) %copy-start.11) | copy-done | bytes 32
  17.6 2.6 %table.1 = (bf16[5,768,512]{2,1,0:T(8,128)(2,1)S(1)}, f32[24,1280]{1,0:T(8,128)S(1)}) custom-call(s32[2]{0:T(128)S(1)} %copy-done.11, s32[1,1280]{1,0:T(1,128)S(1)} %reshape.10.mode_ref), custom_call_target="tpu_custom_call" | custom-call | flops 20000000 | bytes 4000000 | tf_op jit(solution)/shard_map/table/pallas_call | solution.py:351
  20.2 0.0 copy-start.1
  20.2 1.8 %copy-done.1 = bf16[5,768,512]{2,1,0:T(8,128)(2,1)} copy-done((bf16[5,768,512]{2,1,0:T(8,128)(2,1)}, bf16[5,768,512]{2,1,0:T(8,128)(2,1)S(1)}, u32[]{:S(2)}) %copy-start.1) | copy-done | bytes 3932184
  22.0 1.7 %all-to-all-done.grid_ref = bf16[8,32,768]{2,1,0:T(8,128)(2,1)S(1)} async-done(((bf16[8,32,768]{2,1,0:T(8,128)(2,1)}), bf16[8,32,768]{2,1,0:T(8,128)(2,1)S(1)}, u32[]{:S(2)}, u32[]{:S(2)}) %all-to-all-start) | async-done | bytes 393248 | tf_op jit(solution)/shard_map/all_to_all | solution.py:368
  23.7 0.0 copy-start.2
  23.7 2.1 %copy-done.2 = bf16[5,768,512]{2,1,0:T(8,128)(2,1)S(1)} copy-done((bf16[5,768,512]{2,1,0:T(8,128)(2,1)S(1)}, bf16[5,768,512]{2,1,0:T(8,128)(2,1)}, u32[]{:S(2)}) %copy-start.2) | copy-done | bytes 3932184
  25.8 0.0 copy-start.4
  25.8 1.2 %copy-done.4 = bf16[768,640]{1,0:T(8,128)(2,1)S(1)} copy-done((bf16[768,640]{1,0:T(8,128)(2,1)S(1)}, bf16[768,640]{1,0:T(8,128)(2,1)}, u32[]{:S(2)}) %copy-start.4) | copy-done | bytes 983064
  27.0 3.2 %fourier.1 = bf16[32,24,128]{2,1,0:T(8,128)(2,1)S(1)} custom-call(bf16[8,32,768]{2,1,0:T(8,128)(2,1)S(1)} %all-to-all-done.grid_ref, bf16[5,768,512]{2,1,0:T(8,128)(2,1)S(1)} %copy-done.2, f32[24,1280]{1,0:T(8,128)S(1)} %get-tuple-element.8.aux_hbm, bf16[768,640]{1,0:T(8,128)(2,1)S(1)} %copy-done.4), custom_call_target="tpu_custom_call" | custom-call | flops 1000000000 | bytes 5000000 | tf_op jit(solution)/shard_map/fourier/pallas_call | solution.py:369
  30.2 24.0 %all_to_all.10.msg_ref = bf16[32,24,128]{2,1,0:T(8,128)(2,1)S(1)} all-to-all(bf16[32,24,128]{2,1,0:T(8,128)(2,1)S(1)} %fourier.1), channel_id=1, replica_groups=mesh['lat'=32,'lon'=8] {'lat'}, dimensions={0} | all-to-all | bytes 393216 | tf_op jit(solution)/shard_map/all_to_all | solution.py:386
  54.2 0.0 copy-done.3
  54.2 0.0 copy-done.10
  54.2 0.0 copy-start
  54.2 2.9 %copy-done = bf16[40,64,1280]{2,1,0:T(8,128)(2,1)S(1)} copy-done((bf16[40,64,1280]{2,1,0:T(8,128)(2,1)S(1)}, bf16[40,64,1280]{2,1,0:T(8,128)(2,1)}, u32[]{:S(2)}) %copy-start) | copy-done | bytes 6553624
  57.1 6.8 %legendre.1 = bf16[40,2,4,2,1280]{4,3,2,1,0:T(2,128)(2,1)} custom-call(s32[1280]{0:T(1024)S(1)} %copy-done.10, bf16[32,24,128]{2,1,0:T(8,128)(2,1)S(1)} %all_to_all.10.msg_ref, bf16[10,256,1280]{2,1,0:T(8,128)(2,1)S(1)} %bitcast.2, bf16[768,768]{1,0:T(8,128)(2,1)S(1)} %copy-done.3), custom_call_target="tpu_custom_call" | custom-call | flops 500000000 | bytes 8000000 | tf_op jit(solution)/shard_map/legendre/pallas_call | solution.py:389
Async XLA Ops:
  0.0 1.0 %copy-start.5 = (bf16[256,768]{1,0:T(8,128)(2,1)S(1)}, bf16[256,768]{1,0:T(8,128)(2,1)}, u32[]{:S(2)}) copy-start(bf16[256,768]{1,0:T(8,128)(2,1)} %constant.9.clone.order_hbm) | copy-start | bytes 1179652
  1.0 1.0 %copy-start.6 = (f32[4,2,16,640]{3,2,1,0:T(8,128)S(1)}, f32[4,2,16,640]{3,2,1,0:T(8,128)}, u32[]{:S(2)}) copy-start(f32[4,2,16,640]{3,2,1,0:T(8,128)} %grid_hbm.1) | copy-start | bytes 983044
  2.0 1.0 %copy-start.7 = (bf16[192,768]{1,0:T(8,128)(2,1)S(1)}, bf16[192,768]{1,0:T(8,128)(2,1)}, u32[]{:S(2)}) copy-start(bf16[192,768]{1,0:T(8,128)(2,1)} %constant.8.clone.spread_hbm) | copy-start | bytes 884740
  2.9 0.9 %copy-start.8 = (bf16[2,16,4,640]{3,2,1,0:T(4,128)(2,1)S(1)}, bf16[2,16,4,640]{3,2,1,0:T(4,128)(2,1)}, u32[]{:S(2)}) copy-start(bf16[2,16,4,640]{3,2,1,0:T(4,128)(2,1)} %weight_hbm.1) | copy-start | bytes 491524
  3.8 0.9 %copy-start.9 = (s32[2,16,2,640]{3,2,1,0:T(2,128)S(1)}, s32[2,16,2,640]{3,2,1,0:T(2,128)}, u32[]{:S(2)}) copy-start(s32[2,16,2,640]{3,2,1,0:T(2,128)} %offset_hbm.1) | copy-start | bytes 491524
  4.8 49.5 %copy-start.3 = (bf16[768,768]{1,0:T(8,128)(2,1)S(1)}, bf16[768,768]{1,0:T(8,128)(2,1)}, u32[]{:S(2)}) copy-start(bf16[768,768]{1,0:T(8,128)(2,1)} %constant.11.clone.order_hbm) | copy-start | bytes 3538948
  9.7 44.5 %copy-start.10 = (s32[1280]{0:T(1024)S(1)}, s32[1280]{0:T(1024)}, u32[]{:S(2)}) copy-start(s32[1280]{0:T(1024)} %mode_ref.1) | copy-start | bytes 15364
  9.7 14.0 %all-to-all-start = ((bf16[8,32,768]{2,1,0:T(8,128)(2,1)}), bf16[8,32,768]{2,1,0:T(8,128)(2,1)S(1)}, u32[]{:S(2)}, u32[]{:S(2)}) async-start(bf16[8,32,768]{2,1,0:T(8,128)(2,1)} %deposit.1), calls=%async_computation | async-start | bytes 786432 | tf_op jit(solution)/shard_map/all_to_all | solution.py:368
  16.9 0.7 %copy-start.11 = (s32[2]{0:T(128)S(1)}, s32[2]{0:T(128)}, u32[]{:S(2)}) copy-start(s32[2]{0:T(128)} %points_ref.1) | copy-start | bytes 28
  20.2 1.9 %copy-start.1 = (bf16[5,768,512]{2,1,0:T(8,128)(2,1)}, bf16[5,768,512]{2,1,0:T(8,128)(2,1)S(1)}, u32[]{:S(2)}) copy-start(bf16[5,768,512]{2,1,0:T(8,128)(2,1)S(1)} %get-tuple-element.7.table_hbm) | copy-start | bytes 11796484
  23.7 2.1 %copy-start.2 = (bf16[5,768,512]{2,1,0:T(8,128)(2,1)S(1)}, bf16[5,768,512]{2,1,0:T(8,128)(2,1)}, u32[]{:S(2)}) copy-start(bf16[5,768,512]{2,1,0:T(8,128)(2,1)} %copy-done.1) | copy-start | bytes 11796484
  25.8 1.2 %copy-start.4 = (bf16[768,640]{1,0:T(8,128)(2,1)S(1)}, bf16[768,640]{1,0:T(8,128)(2,1)}, u32[]{:S(2)}) copy-start(bf16[768,640]{1,0:T(8,128)(2,1)} %constant.10.clone.order_hbm) | copy-start | bytes 2949124
  54.2 2.9 %copy-start = (bf16[40,64,1280]{2,1,0:T(8,128)(2,1)S(1)}, bf16[40,64,1280]{2,1,0:T(8,128)(2,1)}, u32[]{:S(2)}) copy-start(bf16[40,64,1280]{2,1,0:T(8,128)(2,1)} %param.15) | copy-start | bytes 19660804

commit v3 on v2

--- a/solution.py
+++ b/solution.py
@@ -317,6 +317,10 @@
     return pl.BlockSpec(memory_space=pltpu.VMEM)
 
 
+def hbm(*arrays):
+    return [pltpu.with_memory_space_constraint(x, pltpu.HBM) for x in arrays]
+
+
 def in_hbm():
     return pl.BlockSpec(memory_space=pltpu.HBM)
 
@@ -346,14 +350,14 @@
         ],
         compiler_params=params(14),
         cost_estimate=pl.CostEstimate(flops=20_000_000, bytes_accessed=1_500_000, transcendentals=0),
-    )(grid_cot, weights, offsets, jnp.asarray(spread_order()), jnp.asarray(level_order()))
+    )(*hbm(grid_cot, weights, offsets, jnp.asarray(spread_order()), jnp.asarray(level_order())))
     column_mode = slot_mode.reshape(M // LANE_SLOTS, LANE_SLOTS).T.reshape(1, M)
     table, aux = pl.pallas_call(
         table_kernel,
         name="table",
         out_shape=(
-            jax.ShapeDtypeStruct((BLOCKS, WIDE, 2 * BLOCK), BF16),
-            jax.ShapeDtypeStruct((AUX, M), F32),
+            pltpu.HBM((BLOCKS, WIDE, 2 * BLOCK), BF16),
+            pltpu.HBM((AUX, M), F32),
         ),
         in_specs=[in_smem(), in_vmem()],
         out_specs=(in_hbm(), in_hbm()),
@@ -382,7 +386,7 @@
         ],
         compiler_params=params(14),
         cost_estimate=pl.CostEstimate(flops=1_000_000_000, bytes_accessed=5_000_000, transcendentals=0),
-    )(circles, table, aux, jnp.asarray(message_order()))
+    )(circles, *hbm(table, aux, jnp.asarray(message_order())))
     coefficients = lax.all_to_all(message, "lat", split_axis=0, concat_axis=0, tiled=True)
     shape = (SLOTS, 2, FIELDS, PER_PEER, NL)
     quads = SLOTS // 4
@@ -400,7 +404,7 @@
         ],
         compiler_params=params(20),
         cost_estimate=pl.CostEstimate(flops=500_000_000, bytes_accessed=8_000_000, transcendentals=0),
-    )(slot_mode, coefficients, legendre.reshape(quads, 4 * NLAT, NL), jnp.asarray(latitude_order()))
+    )(slot_mode, coefficients, *hbm(legendre.reshape(quads, 4 * NLAT, NL), jnp.asarray(latitude_order())))
 
 
 def solution(mesh):

time: 64.4 us -> 52.9 us (0.82)
  local copies, waits for them, and re-layouts: 14.4 us -> 1.6 us
  waiting for transfers between devices: 1.68 us -> 3.22 us
    unnamed x24 -> x4, local copies, waits for them, and re-layouts: 13.4 us -> 0.67 us
    all_to_all x1, waiting for transfers between devices: 1.68 us -> 3.22 us  [per_device(): lax.all_to_all(sent, 'lon', split_axis=0, concat_axis=0, tiled=True)]
    pallas_call x1, Pallas kernels: 6.78 us -> 5.74 us  [per_device(): pl.pallas_call(legendre_kernel, name='legendre', out_shape=jax.ShapeDtype...]
  transfers between devices with their start and end apart: 1 -> 1, of which waited for: 1 -> 1; matrix products, arithmetic and copies ran while one was open for 1% -> 2% of each run, Pallas kernels for 4% -> 6%
where the time goes in v3:
time: 52.9 us; the launch traced here: 52.6 us
  blocking collectives  24 us (45%)
  Pallas kernels  17.6 us (33%)
  starting transfers between devices  6.21 us (12%)
  waiting for transfers between devices  3.22 us (6%)
  local copies, waits for them, and re-layouts  1.6 us (3%)
    all_to_all x1, blocking collectives, per_device(): lax.all_to_all(message, 'lat', split_axis=0, concat_axis=0, tiled=True)  24 us
    all_to_all x1, starting transfers between devices, per_device(): lax.all_to_all(sent, 'lon', split_axis=0, concat_axis=0, tiled=True)  6.21 us
    pallas_call x1, Pallas kernels, per_device(): pl.pallas_call(legendre_kernel, name='legendre', out_shape=jax.ShapeDtype...  5.74 us
    pallas_call x1, Pallas kernels, per_device(): pl.pallas_call(deposit_kernel, name='deposit', out_shape=jax.ShapeDtypeSt...  5.21 us
    pallas_call x1, Pallas kernels, per_device(): pl.pallas_call(fourier_kernel, name='fourier', out_shape=jax.ShapeDtypeSt...  3.66 us
    all_to_all x1, waiting for transfers between devices, per_device(): lax.all_to_all(sent, 'lon', split_axis=0, concat_axis=0, tiled=True)  3.22 us
    pallas_call x1, Pallas kernels, per_device(): pl.pallas_call(table_kernel, name='table', out_shape=(pltpu.HBM((BLOCKS,...  2.95 us
  transfers between devices with their start and end apart: 1, of which 1 were waited for; matrix products, arithmetic and copies ran while one was open for 2% of the time, Pallas kernels for 6%

profile of v3, /device:TPU:1, one launch (start us, length us, event | category | flops | bytes accessed | tf_op | source)
XLA Modules:
  0.0 52.6 jit_solution(819618581961788173)
XLA Ops:
  0.0 5.2 %deposit.1 = bf16[8,32,768]{2,1,0:T(8,128)(2,1)} custom-call(f32[4,2,16,640]{3,2,1,0:T(8,128)} %grid_hbm.1, bf16[2,16,4,640]{3,2,1,0:T(4,128)(2,1)} %weight_hbm.1, s32[2,16,2,640]{3,2,1,0:T(2,128)} %offset_hbm.1, bf16[192,768]{1,0:T(8,128)(2,1)} %constant.8.clone.spread_hbm, bf16[256,768]{1,0:T(8,128)(2,1)} %constant.9.clone.order_hbm), custom_call_target="tpu_custom_call" | custom-call | flops 20000000 | bytes 1500000 | tf_op jit(solution)/shard_map/deposit/pallas_call | solution.py:333
  5.2 0.0 copy-start
  5.2 6.2 %all-to-all-start = ((bf16[8,32,768]{2,1,0:T(8,128)(2,1)}), bf16[8,32,768]{2,1,0:T(8,128)(2,1)S(1)}, u32[]{:S(2)}, u32[]{:S(2)}) async-start(bf16[8,32,768]{2,1,0:T(8,128)(2,1)} %deposit.1), calls=%async_computation | async-start | bytes 786432 | tf_op jit(solution)/shard_map/all_to_all | solution.py:372
  11.4 0.8 %reshape.9 = s32[160,8]{1,0:T(8,128)S(1)} reshape(s32[1280]{0:T(1024)} %mode_ref.1) | data formatting | bytes 10240 | tf_op jit(solution)/shard_map/reshape | solution.py:354
  12.2 0.1 copy.11
  12.3 0.1 reshape.10.mode_ref
  12.4 0.0 copy-start.1
  12.4 0.7 %copy-done.1 = s32[2]{0:T(128)S(1)} copy-done((s32[2]{0:T(128)S(1)}, s32[2]{0:T(128)}, u32[]{:S(2)}) %copy-start.1) | copy-done | bytes 32
  13.1 2.9 %table.1 = (bf16[5,768,512]{2,1,0:T(8,128)(2,1)}, f32[24,1280]{1,0:T(8,128)}) custom-call(s32[2]{0:T(128)S(1)} %copy-done.1, s32[1,1280]{1,0:T(1,128)S(1)} %reshape.10.mode_ref), custom_call_target="tpu_custom_call" | custom-call | flops 20000000 | bytes 4000000 | tf_op jit(solution)/shard_map/table/pallas_call | solution.py:355
  16.0 3.2 %all-to-all-done.grid_ref = bf16[8,32,768]{2,1,0:T(8,128)(2,1)S(1)} async-done(((bf16[8,32,768]{2,1,0:T(8,128)(2,1)}), bf16[8,32,768]{2,1,0:T(8,128)(2,1)S(1)}, u32[]{:S(2)}, u32[]{:S(2)}) %all-to-all-start) | async-done | bytes 393248 | tf_op jit(solution)/shard_map/all_to_all | solution.py:372
  19.2 3.7 %fourier.1 = bf16[32,24,128]{2,1,0:T(8,128)(2,1)S(1)} custom-call(bf16[8,32,768]{2,1,0:T(8,128)(2,1)S(1)} %all-to-all-done.grid_ref, bf16[5,768,512]{2,1,0:T(8,128)(2,1)} %get-tuple-element.7.table_hbm, f32[24,1280]{1,0:T(8,128)} %get-tuple-element.8.aux_hbm, bf16[768,640]{1,0:T(8,128)(2,1)} %constant.10.clone.order_hbm), custom_call_target="tpu_custom_call" | custom-call | flops 1000000000 | bytes 5000000 | tf_op jit(solution)/shard_map/fourier/pallas_call | solution.py:373
  22.9 24.0 %all_to_all.10.msg_ref = bf16[32,24,128]{2,1,0:T(8,128)(2,1)S(1)} all-to-all(bf16[32,24,128]{2,1,0:T(8,128)(2,1)S(1)} %fourier.1), channel_id=1, replica_groups=mesh['lat'=32,'lon'=8] {'lat'}, dimensions={0} | all-to-all | bytes 393216 | tf_op jit(solution)/shard_map/all_to_all | solution.py:390
  46.9 0.0 copy-done
  46.9 5.7 %legendre.1 = bf16[40,2,4,2,1280]{4,3,2,1,0:T(2,128)(2,1)} custom-call(s32[1280]{0:T(1024)S(1)} %copy-done, bf16[32,24,128]{2,1,0:T(8,128)(2,1)S(1)} %all_to_all.10.msg_ref, bf16[10,256,1280]{2,1,0:T(8,128)(2,1)} %bitcast.2, bf16[768,768]{1,0:T(8,128)(2,1)} %constant.11.clone.order_hbm), custom_call_target="tpu_custom_call" | custom-call | flops 500000000 | bytes 8000000 | tf_op jit(solution)/shard_map/legendre/pallas_call | solution.py:393
Async XLA Ops:
  5.2 41.7 %copy-start = (s32[1280]{0:T(1024)S(1)}, s32[1280]{0:T(1024)}, u32[]{:S(2)}) copy-start(s32[1280]{0:T(1024)} %mode_ref.1) | copy-start | bytes 15364
  5.2 14.0 %all-to-all-start = ((bf16[8,32,768]{2,1,0:T(8,128)(2,1)}), bf16[8,32,768]{2,1,0:T(8,128)(2,1)S(1)}, u32[]{:S(2)}, u32[]{:S(2)}) async-start(bf16[8,32,768]{2,1,0:T(8,128)(2,1)} %deposit.1), calls=%async_computation | async-start | bytes 786432 | tf_op jit(solution)/shard_map/all_to_all | solution.py:372
  12.4 0.7 %copy-start.1 = (s32[2]{0:T(128)S(1)}, s32[2]{0:T(128)}, u32[]{:S(2)}) copy-start(s32[2]{0:T(128)} %points_ref.1) | copy-start | bytes 28

commit v4 on v3

v4 whole, which is shorter than its diff:
```python
import functools

import jax
import jax.numpy as jnp
import numpy as np
from jax import lax
from jax.experimental import pallas as pl
from jax.experimental.pallas import tpu as pltpu
from jax.sharding import PartitionSpec as P

FIELDS = 4
NLON = 5120
M = 1280
NL = 1280
REACH = 4
LEV = 16
ROWS = 2
TARGETS = ROWS + 2
SECTORS = 8
BANDS = 32
COLS = NLON // SECTORS
WIDE = 768
PER_PEER = LEV // SECTORS
LINES = TARGETS * FIELDS * PER_PEER
SLOTS = M // BANDS
LANE_SLOTS = 8
GROUPS = SLOTS // LANE_SLOTS
MSG = TARGETS * (GROUPS + 1)
NLAT = ROWS * BANDS

F32 = jnp.float32
BF16 = jnp.bfloat16


def dot(a, b, dims):
    return lax.dot_general(a, b, (dims, ((), ())), preferred_element_type=F32)


def one_hot(target, rows):
    row = lax.broadcasted_iota(jnp.int32, (rows, target.shape[1]), 0)
    return jnp.where(row == target, 1.0, 0.0).astype(BF16)


def spread_order():
    lane = lax.broadcasted_iota(jnp.int32, (1, 6 * LANES), 1)
    kind = lane // LANES
    place = (lane // (FIELDS * LEV)) % ROWS * LEV + lane % LEV
    return one_hot(jnp.where(kind < 4, place * 4 + kind, ROWS * LEV * 4 + place * 2 + kind - 4), 6 * ROWS * LEV)


def line_order():
    lane = lax.broadcasted_iota(jnp.int32, (1, 2 * LANES), 1)
    half = lane // (FIELDS * LEV) % 2
    target = jnp.where(lane < LANES, half * 3, half + 1)
    field = lane // LEV % FIELDS
    level = lane % LEV
    row = ((level // PER_PEER * TARGETS + target) * FIELDS + field) * PER_PEER + level % PER_PEER
    return one_hot(row, SECTORS * LINES)


UNROLL = 32
LANES = FIELDS * ROWS * LEV


def deposit_kernel(
    grid_hbm, weight_hbm, offset_hbm, out_ref, grid, weight, offset, sems, stacked, wide, terms, sums, parts
):
    pairs = ((offset_hbm, offset), (weight_hbm, weight), (grid_hbm, grid))
    copies = [pltpu.make_async_copy(src, dst, sems.at[n]) for n, (src, dst) in enumerate(pairs)]
    for copy in copies:
        copy.start()
    spread = spread_order()
    order = line_order()
    for n in range(7):
        fill = jnp.full((8, LANES), 99.0 if n == 0 else 0.0, F32)
        terms[n, 0:8] = fill
        terms[n, COLS + 8 : COLS + 16] = fill
    copies[0].wait()
    for i in range(ROWS):
        for v in range(LEV):
            at = ROWS * LEV * 4 + (i * LEV + v) * 2
            stacked[at : at + 2, :] = offset[i, v].astype(F32)
    copies[1].wait()
    for i in range(ROWS):
        for v in range(LEV):
            at = (i * LEV + v) * 4
            stacked[at : at + 4, :] = weight[i, v].astype(F32)
    wide[...] = dot(stacked[...].astype(BF16), spread, ((0,), (0,)))
    copies[2].wait()
    for j in range(COLS // 128):
        rows = slice(128 * j, 128 * j + 128)
        lines = slice(128 * j + 8, 128 * j + 136)
        g = jnp.concatenate([grid[:, i, :, rows].reshape(FIELDS * LEV, 128) for i in range(ROWS)], axis=0).T
        w = [g * wide[rows, c * LANES : (c + 1) * LANES] for c in range(4)]
        south = wide[rows, 4 * LANES : 5 * LANES] < -0.5
        terms[0, lines] = wide[rows, 5 * LANES :]
        for q in range(2):
            terms[1 + q, lines] = jnp.where(south, w[q], 0.0)
            terms[3 + q, lines] = jnp.where(south, w[2 + q], w[q])
            terms[5 + q, lines] = jnp.where(south, 0.0, w[2 + q])

    def tile(start):
        total = [jnp.zeros((8, LANES), F32) for _ in range(3)]
        for n in range(2 * REACH + 1):
            shift = REACH - n
            east = terms[0, pl.ds(start + n, 8), :]
            here = east == float(shift)
            before = east == float(shift - 1)
            for r in range(3):
                first = terms[1 + 2 * r, pl.ds(start + n, 8), :]
                second = terms[2 + 2 * r, pl.ds(start + n, 8), :]
                total[r] = total[r] + jnp.where(here, first, jnp.where(before, second, 0.0))
        return total

    def step(n, carry):
        start = pl.multiple_of(n * UNROLL, UNROLL)
        for m in range(0, UNROLL, 8):
            for r, total in enumerate(tile(start + m)):
                sums[r, pl.ds(start + m, 8), :] = total
        return carry

    lax.fori_loop(0, COLS // UNROLL, step, 0)
    for r, total in enumerate(tile(COLS)):
        sums[r, COLS : COLS + 8] = total
        sums[r, COLS + 8 :] = jnp.zeros((WIDE - COLS - 8, LANES), F32)
    north, same, south = sums[0], sums[1], sums[2]
    inner = lax.broadcasted_iota(jnp.int32, (1, LANES), 1) < FIELDS * LEV
    parts[:, :LANES] = jnp.where(inner, north, south).astype(BF16)
    parts[:, LANES:] = (same + pltpu.roll(jnp.where(inner, south, north), FIELDS * LEV, 1)).astype(BF16)
    ordered = dot(order, parts[...], ((1,), (1,)))
    out_ref[...] = ordered.astype(BF16).reshape(out_ref.shape)


def sincos(count):
    turn = count - NLON * jnp.round(count * (1.0 / NLON))
    quarter = jnp.round(turn * (4.0 / NLON))
    x = (turn - (NLON // 4) * quarter) * np.float32(2.0 * np.pi / NLON)
    y = x * x
    s = x * (1.0 + y * (-1.0 / 6 + y * (1.0 / 120 + y * (-1.0 / 5040 + y * (1.0 / 362880)))))
    c = 1.0 + y * (-1.0 / 2 + y * (1.0 / 24 + y * (-1.0 / 720 + y * (1.0 / 40320))))
    odd = jnp.abs(quarter) == 1.0
    cosine = jnp.where(odd, s, c)
    sine = jnp.where(odd, c, s)
    cosine = jnp.where((quarter == 1.0) | (jnp.abs(quarter) == 2.0), -cosine, cosine)
    sine = jnp.where((quarter == -1.0) | (jnp.abs(quarter) == 2.0), -sine, sine)
    return cosine, sine


STEP = 16
DEPTH = COLS + STEP
BLOCK = 256
BLOCKS = M // BLOCK
EARLY = 4
AUX = 24


def table_kernel(points_ref, mode_ref, *refs):
    early, (aux, table_hbm, late, sems) = refs[:EARLY], refs[EARLY:]
    table = [*early, *[late.at[n] for n in range(BLOCKS - EARLY)]]
    copies = []
    mode = mode_ref[...].astype(F32)

    def rows(count, scale, first):
        index = lax.broadcasted_iota(jnp.int32, (count, M), 0) * scale + first
        return sincos(index.astype(F32) * mode)

    coarse_c, coarse_s = rows(DEPTH // STEP, STEP, 0)
    fine_c, fine_s = rows(STEP, 1, -REACH)
    factor = jnp.where(mode == 0.0, 1.0, 2.0)
    fine_c = fine_c * factor
    fine_s = fine_s * factor
    for n in (*range(EARLY, BLOCKS), *range(EARLY)):
        part = slice(n * BLOCK, (n + 1) * BLOCK)
        for a in range(DEPTH // STEP):
            c = coarse_c[a : a + 1, part]
            s = coarse_s[a : a + 1, part]
            lines = slice(a * STEP, (a + 1) * STEP)
            table[n][lines, :BLOCK] = (c * fine_c[:, part] - s * fine_s[:, part]).astype(BF16)
            table[n][lines, BLOCK:] = (-s * fine_c[:, part] - c * fine_s[:, part]).astype(BF16)
        if n >= EARLY:
            copies.append(pltpu.make_async_copy(table[n], table_hbm.at[n - EARLY], sems.at[n - EARLY]))
            copies[-1].start()
    turn_c, turn_s = rows(SECTORS, COLS, 0)
    aux[0:SECTORS, :] = turn_c
    aux[SECTORS : 2 * SECTORS, :] = turn_s
    row = lax.broadcasted_iota(jnp.int32, (AUX - 2 * SECTORS, M), 0)
    lane = lax.broadcasted_iota(jnp.int32, (AUX - 2 * SECTORS, M), 1)
    extra = jnp.zeros((AUX - 2 * SECTORS, M), F32)
    for i in range(ROWS):
        count = (points_ref[i] + 1) // 2
        high = count // 16
        value = jnp.where(lane == 0, high, jnp.where(lane == 1, count - 16 * high, 0))
        extra = extra + jnp.where(row == i, value, 0).astype(F32)
    aux[2 * SECTORS :, :] = extra
    for copy in copies:
        copy.wait()


def fourier_kernel(grid_ref, *refs):
    early, (aux, table_hbm, out_ref, late, sem, spectra, lanes, rows) = refs[:EARLY], refs[EARLY:]
    table = [*early, *[late.at[n] for n in range(BLOCKS - EARLY)]]
    copy = pltpu.make_async_copy(table_hbm, late, sem)
    copy.start()
    data = grid_ref[...].reshape(SECTORS * LINES, WIDE)[:, :DEPTH]
    for n in range(BLOCKS):
        part = slice(n * BLOCK, (n + 1) * BLOCK)
        if n == EARLY:
            copy.wait()
        real = dot(data, table[n][:, :BLOCK], ((1,), (0,)))
        imag = dot(data, table[n][:, BLOCK:], ((1,), (0,)))
        sum_r = jnp.zeros((LINES, BLOCK), F32)
        sum_i = jnp.zeros((LINES, BLOCK), F32)
        for j in range(SECTORS):
            c = aux[j : j + 1, part]
            s = aux[SECTORS + j : SECTORS + j + 1, part]
            re = real[j * LINES : (j + 1) * LINES]
            im = imag[j * LINES : (j + 1) * LINES]
            sum_r = sum_r + c * re + s * im
            sum_i = sum_i + c * im - s * re
        for t in range(TARGETS):
            here = slice(8 * t, 8 * t + 8)
            spectra[t, :, part] = jnp.concatenate([sum_r[here], sum_i[here]], axis=0).astype(BF16)
    run = BANDS * GROUPS
    for t in range(TARGETS):
        for b in range(LANE_SLOTS):
            lanes[16 * b : 16 * b + 16, t * run : (t + 1) * run] = spectra[t, :, b * run : (b + 1) * run]
    turned = lanes[...].astype(F32).T
    for t in range(TARGETS):
        for g in range(GROUPS):
            at = (t * GROUPS + g) * BANDS
            rows[pl.ds(t * (GROUPS + 1) + g, BANDS, stride=MSG), :] = turned[at : at + BANDS]
        limit = jnp.zeros((BANDS, 128), F32)
        if 0 < t <= ROWS:
            limit = limit + aux[2 * SECTORS + t - 1 : 2 * SECTORS + t, 0:128]
        rows[pl.ds(t * (GROUPS + 1) + GROUPS, BANDS, stride=MSG), :] = limit
    out_ref[...] = rows[...].astype(BF16).reshape(out_ref.shape)


QUADS = SLOTS // 4
STAGED = 5
CUT = 8


def stage_kernel(legendre_hbm, *refs):
    *legendre, sems = refs
    copies = [pltpu.make_async_copy(legendre_hbm.at[q], legendre[q], sems.at[q]) for q in range(STAGED)]
    for copy in copies:
        copy.start()
    for copy in copies:
        copy.wait()


def legendre_kernel(mode_ref, msg_ref, *refs):
    early, (legendre_hbm, out_hbm, late, out, late_sems, sems, rows, mixed) = refs[:STAGED], refs[STAGED:]
    legendre = [*early, *[late.at[q] for q in range(QUADS - STAGED)]]
    copies = {
        first: pltpu.make_async_copy(
            legendre_hbm.at[pl.ds(first, last - first)], late.at[pl.ds(first - STAGED, last - first)], late_sems.at[n]
        )
        for n, (first, last) in enumerate(((STAGED, CUT), (CUT, QUADS)))
    }
    for copy in copies.values():
        copy.start()
    base = lax.axis_index("lat") * SLOTS
    rows[0:MSG] = jnp.zeros((MSG, 128), F32)
    rows[MSG : (BANDS + 1) * MSG] = msg_ref[...].reshape(BANDS * MSG, 128).astype(F32)
    rows[(BANDS + 1) * MSG :] = jnp.zeros((MSG, 128), F32)
    for g in range(GROUPS + 1):

        def part(t, neighbour):
            return rows[pl.ds((1 + neighbour) * MSG + t * (GROUPS + 1) + g, BANDS, stride=MSG), :]

        mixed[pl.ds(g * NLAT, BANDS, stride=2), :] = part(1, 0) + part(3, -1)
        mixed[pl.ds(g * NLAT + 1, BANDS, stride=2), :] = part(2, 0) + part(0, 1)
    spread = mixed[...].T
    lane = lax.broadcasted_iota(jnp.int32, (16, 128), 1)
    first = lane < NLAT
    plain = [spread[:, 128 * p : 128 * p + 128] for p in range((GROUPS + 1) // 2)]
    swapped = [pltpu.roll(p, NLAT, 1) for p in plain]
    limit = jnp.where(
        first[0:1],
        16.0 * swapped[-1][0:1] + swapped[-1][1:2],
        16.0 * plain[-1][0:1] + plain[-1][1:2],
    )
    degree = lax.broadcasted_iota(jnp.int32, (16, NL), 1)
    none = jnp.zeros((16, 128), F32)
    sent = []
    for q in range(QUADS):
        g, half = divmod(q, 2)
        left = []
        for n in range(4):
            b = 4 * half + n
            mode = mode_ref[base + g * LANE_SLOTS + b]
            keep = mode.astype(F32) < limit
            own = first if n % 2 == 0 else ~first
            value = (plain if g % 2 == n % 2 else swapped)[g // 2][16 * b : 16 * b + 16]
            value = jnp.where(keep & own, value, none)
            left.append(jnp.concatenate([value, none] if n < 2 else [none, value], axis=1))
        left = jnp.concatenate(left, axis=0).astype(BF16)
        if q in copies:
            copies[q].wait()
        result = dot(left, legendre[q][...], ((1,), (0,)))
        for n in range(4):
            slot = 4 * q + n
            mode = mode_ref[base + slot]
            block = jnp.where(degree >= mode, result[16 * n : 16 * n + 16], 0.0)
            for r in range(2):
                for f in range(FIELDS):
                    at = (r * FIELDS + f) * PER_PEER
                    out[slot, r, f] = block[at : at + PER_PEER].astype(BF16)
        here = pl.ds(4 * q, 4)
        sent.append(pltpu.make_async_copy(out.at[here], out_hbm.at[here], sems.at[q]))
        sent[-1].start()
    for copy in sent:
        copy.wait()


def params(mib):
    return pltpu.CompilerParams(vmem_limit_bytes=mib * 1024 * 1024)


def in_vmem():
    return pl.BlockSpec(memory_space=pltpu.VMEM)


def hbm(*arrays):
    return [pltpu.with_memory_space_constraint(x, pltpu.HBM) for x in arrays]


def vmem(*arrays):
    return [pltpu.with_memory_space_constraint(x, pltpu.VMEM) for x in arrays]


def in_hbm():
    return pl.BlockSpec(memory_space=pltpu.HBM)


def in_smem():
    return pl.BlockSpec(memory_space=pltpu.SMEM)


def per_device(grid_cot, weights, offsets, lat_points, slot_mode, legendre):
    sent = pl.pallas_call(
        deposit_kernel,
        name="deposit",
        out_shape=pltpu.VMEM((SECTORS, LINES, WIDE), BF16),
        in_specs=[in_hbm()] * 3,
        out_specs=in_vmem(),
        scratch_shapes=[
            pltpu.VMEM(grid_cot.shape, F32),
            pltpu.VMEM(weights.shape, BF16),
            pltpu.VMEM(offsets.shape, jnp.int32),
            pltpu.SemaphoreType.DMA((3,)),
            pltpu.VMEM((6 * ROWS * LEV, COLS), F32),
            pltpu.VMEM((COLS, 6 * LANES), F32),
            pltpu.VMEM((7, COLS + 16, LANES), F32),
            pltpu.VMEM((3, WIDE, LANES), F32),
            pltpu.VMEM((WIDE, 2 * LANES), BF16),
        ],
        compiler_params=params(14),
        cost_estimate=pl.CostEstimate(flops=20_000_000, bytes_accessed=1_500_000, transcendentals=0),
    )(*hbm(grid_cot, weights, offsets))
    column_mode = slot_mode.reshape(BANDS, GROUPS, LANE_SLOTS).transpose(2, 1, 0).reshape(1, M)
    *tables, table_rest = pl.pallas_call(
        table_kernel,
        name="table",
        out_shape=(
            *[pltpu.VMEM((DEPTH, 2 * BLOCK), BF16)] * EARLY,
            pltpu.VMEM((AUX, M), F32),
            pltpu.HBM((BLOCKS - EARLY, DEPTH, 2 * BLOCK), BF16),
        ),
        in_specs=[in_smem(), in_vmem()],
        out_specs=(*[in_vmem()] * (EARLY + 1), in_hbm()),
        scratch_shapes=[
            pltpu.VMEM((BLOCKS - EARLY, DEPTH, 2 * BLOCK), BF16),
            pltpu.SemaphoreType.DMA((BLOCKS - EARLY,)),
        ],
        compiler_params=params(12),
        cost_estimate=pl.CostEstimate(flops=20_000_000, bytes_accessed=4_000_000, transcendentals=0),
    )(lat_points, column_mode)
    circles = lax.all_to_all(sent, "lon", split_axis=0, concat_axis=0, tiled=True)
    message = pl.pallas_call(
        fourier_kernel,
        name="fourier",
        out_shape=pltpu.VMEM((BANDS, MSG, 128), BF16),
        in_specs=[in_vmem()] * (EARLY + 2) + [in_hbm()],
        out_specs=in_vmem(),
        scratch_shapes=[
            pltpu.VMEM((BLOCKS - EARLY, DEPTH, 2 * BLOCK), BF16),
            pltpu.SemaphoreType.DMA,
            pltpu.VMEM((TARGETS, 16, M), BF16),
            pltpu.VMEM((128, TARGETS * BANDS * GROUPS), BF16),
            pltpu.VMEM((BANDS * MSG, 128), F32),
        ],
        compiler_params=params(14),
        cost_estimate=pl.CostEstimate(flops=1_000_000_000, bytes_accessed=5_000_000, transcendentals=0),
    )(circles, *vmem(*tables), *hbm(table_rest))
    shape = (SLOTS, 2, FIELDS, PER_PEER, NL)
    message, legendre = lax.optimization_barrier((message, legendre.reshape(QUADS, 4 * NLAT, NL)))
    staged = pl.pallas_call(
        stage_kernel,
        name="stage",
        out_shape=(
            *[pltpu.VMEM((4 * NLAT, NL), BF16)] * STAGED,
        ),
        in_specs=[in_hbm()],
        out_specs=(in_vmem(),) * STAGED,
        scratch_shapes=[pltpu.SemaphoreType.DMA((STAGED,))],
        compiler_params=params(12),
        cost_estimate=pl.CostEstimate(flops=0, bytes_accessed=16_000_000, transcendentals=0),
    )(*hbm(legendre))
    coefficients = lax.all_to_all(message, "lat", split_axis=0, concat_axis=0, tiled=True)
    return pl.pallas_call(
        legendre_kernel,
        name="legendre",
        out_shape=jax.ShapeDtypeStruct(shape, BF16),
        in_specs=[in_smem()] + [in_vmem()] * (STAGED + 1) + [in_hbm()],
        out_specs=in_hbm(),
        scratch_shapes=[
            pltpu.VMEM((QUADS - STAGED, 4 * NLAT, NL), BF16),
            pltpu.VMEM(shape, BF16),
            pltpu.SemaphoreType.DMA((2,)),
            pltpu.SemaphoreType.DMA((QUADS,)),
            pltpu.VMEM(((BANDS + 2) * MSG, 128), F32),
            pltpu.VMEM(((GROUPS + 1) * NLAT, 128), F32),
        ],
        compiler_params=params(12),
        cost_estimate=pl.CostEstimate(flops=500_000_000, bytes_accessed=8_000_000, transcendentals=0),
    )(slot_mode, coefficients, *vmem(*staged), *hbm(legendre))


def solution(mesh):
    placed = (
        P(None, "lat", None, "lon"),
        P("lat", None, None, "lon"),
        P("lat", None, None, "lon"),
        P("lat"),
        P(),
        P("lat", None, None),
    )
    return jax.shard_map(
        per_device,
        mesh=mesh,
        in_specs=placed,
        out_specs=P("lat", None, None, "lon", None),
        check_vma=False,
    )
```

time: 52.9 us -> 50.8 us (0.960)
  blocking collectives: 24 us -> 0 us
  starting transfers between devices: 6.21 us -> 18.4 us
  waiting for transfers between devices: 3.22 us -> 14.1 us
  Pallas kernels: 17.6 us -> 16.1 us
    all_to_all x1 -> x0, blocking collectives: 24 us -> none  [per_device(): lax.all_to_all(message, 'lat', split_axis=0, concat_axis=0, tiled=True)]
    all_to_all x0 -> x1, starting transfers between devices: none -> 12.2 us  [per_device(): lax.all_to_all(message, 'lat', split_axis=0, concat_axis=0, tiled=True)]
    all_to_all x0 -> x1, waiting for transfers between devices: none -> 10 us  [per_device(): lax.all_to_all(message, 'lat', split_axis=0, concat_axis=0, tiled=True)]
    pallas_call x1, Pallas kernels: 5.74 us -> 4.65 us  [per_device(): pl.pallas_call(legendre_kernel, name='legendre', out_shape=jax.ShapeDtype...]
    all_to_all x1, waiting for transfers between devices: 3.22 us -> 4.12 us  [per_device(): lax.all_to_all(sent, 'lon', split_axis=0, concat_axis=0, tiled=True)]
    pallas_call x3 -> x4, Pallas kernels: 11.8 us -> 11.4 us  [the longest x1 4.38 us: per_device(): pl.pallas_call(deposit_kernel, name='deposit', out_shape=pltpu.VMEM((SECT...]
  transfers between devices with their start and end apart: 1 -> 2, of which waited for: 1 -> 2; matrix products, arithmetic and copies ran while one was open for 2% -> 2% of each run, Pallas kernels for 6% -> 8%
where the time goes in v4:
time: 50.8 us; the launch traced here: 50.4 us
  starting transfers between devices  18.4 us (36%)
  Pallas kernels  16.1 us (32%)
  waiting for transfers between devices  14.1 us (28%)
  local copies, waits for them, and re-layouts  1.65 us (3%)
    all_to_all x1, starting transfers between devices, per_device(): lax.all_to_all(message, 'lat', split_axis=0, concat_axis=0, tiled=True)  12.2 us
    all_to_all x1, waiting for transfers between devices, per_device(): lax.all_to_all(message, 'lat', split_axis=0, concat_axis=0, tiled=True)  10 us
    all_to_all x1, starting transfers between devices, per_device(): lax.all_to_all(sent, 'lon', split_axis=0, concat_axis=0, tiled=True)  6.22 us
    pallas_call x1, Pallas kernels, per_device(): pl.pallas_call(legendre_kernel, name='legendre', out_shape=jax.ShapeDtype...  4.65 us
    pallas_call x1, Pallas kernels, per_device(): pl.pallas_call(deposit_kernel, name='deposit', out_shape=pltpu.VMEM((SECT...  4.38 us
    all_to_all x1, waiting for transfers between devices, per_device(): lax.all_to_all(sent, 'lon', split_axis=0, concat_axis=0, tiled=True)  4.12 us
    pallas_call x1, Pallas kernels, per_device(): pl.pallas_call(fourier_kernel, name='fourier', out_shape=pltpu.VMEM((BAND...  3.14 us
    pallas_call x1, Pallas kernels, per_device(): pl.pallas_call(table_kernel, name='table', out_shape=(*[pltpu.VMEM((DEPTH...  2 us
  transfers between devices with their start and end apart: 2, of which 2 were waited for; matrix products, arithmetic and copies ran while one was open for 2% of the time, Pallas kernels for 8%

profile of v4, /device:TPU:1, one launch (start us, length us, event | category | flops | bytes accessed | tf_op | source)
XLA Modules:
  0.0 50.4 jit_solution(15428633559711439079)
XLA Ops:
  0.0 0.0 copy-start
  0.0 4.4 %deposit.1 = bf16[8,32,768]{2,1,0:T(8,128)(2,1)} custom-call(f32[4,2,16,640]{3,2,1,0:T(8,128)} %grid_hbm.1, bf16[2,16,4,640]{3,2,1,0:T(4,128)(2,1)} %weight_hbm.1, s32[2,16,2,640]{3,2,1,0:T(2,128)} %offset_hbm.1), custom_call_target="tpu_custom_call" | custom-call | flops 20000000 | bytes 1500000 | tf_op jit(solution)/shard_map/deposit/pallas_call | solution.py:343
  4.4 6.2 %all-to-all-start = ((bf16[8,32,768]{2,1,0:T(8,128)(2,1)}), bf16[8,32,768]{2,1,0:T(8,128)(2,1)S(1)}, u32[]{:S(2)}, u32[]{:S(2)}) async-start(bf16[8,32,768]{2,1,0:T(8,128)(2,1)} %deposit.1), calls=%async_computation | async-start | bytes 786432 | tf_op jit(solution)/shard_map/all_to_all | solution.py:381
  10.6 0.8 %reshape.9 = s32[32,5,8]{2,1,0:T(8,128)S(1)} reshape(s32[1280]{0:T(1024)} %mode_ref.1) | data formatting | bytes 10240 | tf_op jit(solution)/shard_map/reshape | solution.py:363
  11.4 0.1 copy.7
  11.5 0.1 reshape.10.mode_ref
  11.6 0.0 copy-start.1
  11.6 0.7 %copy-done.1 = s32[2]{0:T(128)S(1)} copy-done((s32[2]{0:T(128)S(1)}, s32[2]{0:T(128)}, u32[]{:S(2)}) %copy-start.1) | copy-done | bytes 32
  12.3 2.0 %table.1 = (bf16[656,512]{1,0:T(8,128)(2,1)S(1)}, bf16[656,512]{1,0:T(8,128)(2,1)S(1)}, bf16[656,512]{1,0:T(8,128)(2,1)S(1)}, bf16[656,512]{1,0:T(8,128)(2,1)S(1...) custom-call(s32[2]{0:T(128)S(1)} %copy-done.1, s32[1,1280]{1,0:T(1,128)S(1)} %reshape.10.mode_ref), custom_call_target="tpu_custom_call" | custom-call | flops 20000000 | bytes 4000000 | tf_op jit(solution)/shard_map/table/pallas_call | solution.py:364
  14.3 4.1 %all-to-all-done.grid_ref = bf16[8,32,768]{2,1,0:T(8,128)(2,1)S(1)} async-done(((bf16[8,32,768]{2,1,0:T(8,128)(2,1)}), bf16[8,32,768]{2,1,0:T(8,128)(2,1)S(1)}, u32[]{:S(2)}, u32[]{:S(2)}) %all-to-all-start) | async-done | bytes 393248 | tf_op jit(solution)/shard_map/all_to_all | solution.py:381
  18.4 3.1 %fourier.1 = bf16[32,24,128]{2,1,0:T(8,128)(2,1)} custom-call(bf16[8,32,768]{2,1,0:T(8,128)(2,1)S(1)} %all-to-all-done.grid_ref, bf16[656,512]{1,0:T(8,128)(2,1)S(1)} %get-tuple-element.18.refs_0_, bf16[656,512]{1,0:T(8,128)(2,1)S(1)} %get-tuple-element.19.refs_1_, bf16[656,512]{1,0:T(8,128)(2,1)S(1)} %get-tuple-element.20.refs_2_, ...), custom_call_target="tpu_custom_call" | custom-call | flops 1000000000 | bytes 5000000 | tf_op jit(solution)/shard_map/fourier/pallas_call | solution.py:382
  21.5 12.2 %all-to-all-start.1 = ((bf16[32,24,128]{2,1,0:T(8,128)(2,1)}), bf16[32,24,128]{2,1,0:T(8,128)(2,1)S(1)}, u32[]{:S(2)}, u32[]{:S(2)}) async-start(bf16[32,24,128]{2,1,0:T(8,128)(2,1)} %fourier.1), calls=%async_computation.1 | async-start | bytes 393216 | tf_op jit(solution)/shard_map/all_to_all | solution.py:412
  33.8 1.9 %stage.1 = (bf16[256,1280]{1,0:T(8,128)(2,1)S(1)}, bf16[256,1280]{1,0:T(8,128)(2,1)S(1)}, bf16[256,1280]{1,0:T(8,128)(2,1)S(1)}, bf16[256,1280]{1,0:T(8,128)(2,1)S(1)}, bf16[256,1280]{1,0:T(8,128)(2,1)S(1)}) custom-call(bf16[10,256,1280]{2,1,0:T(8,128)(2,1)} %bitcast.2), custom_call_target="tpu_custom_call" | custom-call | bytes 16000000 | tf_op jit(solution)/shard_map/stage/pallas_call | solution.py:400
  35.7 10.0 %all-to-all-done.1.msg_ref = bf16[32,24,128]{2,1,0:T(8,128)(2,1)S(1)} async-done(((bf16[32,24,128]{2,1,0:T(8,128)(2,1)}), bf16[32,24,128]{2,1,0:T(8,128)(2,1)S(1)}, u32[]{:S(2)}, u32[]{:S(2)}) %all-to-all-start.1) | async-done | bytes 196640 | tf_op jit(solution)/shard_map/all_to_all | solution.py:412
  45.7 0.0 copy-done
  45.7 4.7 %legendre.1 = bf16[40,2,4,2,1280]{4,3,2,1,0:T(2,128)(2,1)} custom-call(s32[1280]{0:T(1024)S(1)} %copy-done, bf16[32,24,128]{2,1,0:T(8,128)(2,1)S(1)} %all-to-all-done.1.msg_ref, bf16[256,1280]{1,0:T(8,128)(2,1)S(1)} %get-tuple-element.26.refs_0_, bf16[256,1280]{1,0:T(8,128)(2,1)S(1)} %get-tuple-element.27.refs_1_, ...), custom_call_target="tpu_custom_call" | custom-call | flops 500000000 | bytes 8000000 | tf_op jit(solution)/shard_map/legendre/pallas_call | solution.py:413
Async XLA Ops:
  0.0 45.7 %copy-start = (s32[1280]{0:T(1024)S(1)}, s32[1280]{0:T(1024)}, u32[]{:S(2)}) copy-start(s32[1280]{0:T(1024)} %mode_ref.1) | copy-start | bytes 15364
  4.4 14.0 %all-to-all-start = ((bf16[8,32,768]{2,1,0:T(8,128)(2,1)}), bf16[8,32,768]{2,1,0:T(8,128)(2,1)S(1)}, u32[]{:S(2)}, u32[]{:S(2)}) async-start(bf16[8,32,768]{2,1,0:T(8,128)(2,1)} %deposit.1), calls=%async_computation | async-start | bytes 786432 | tf_op jit(solution)/shard_map/all_to_all | solution.py:381
  11.6 0.7 %copy-start.1 = (s32[2]{0:T(128)S(1)}, s32[2]{0:T(128)}, u32[]{:S(2)}) copy-start(s32[2]{0:T(128)} %points_ref.1) | copy-start | bytes 28
  21.5 24.2 %all-to-all-start.1 = ((bf16[32,24,128]{2,1,0:T(8,128)(2,1)}), bf16[32,24,128]{2,1,0:T(8,128)(2,1)S(1)}, u32[]{:S(2)}, u32[]{:S(2)}) async-start(bf16[32,24,128]{2,1,0:T(8,128)(2,1)} %fourier.1), calls=%async_computation.1 | async-start | bytes 393216 | tf_op jit(solution)/shard_map/all_to_all | solution.py:412

commit v5 on v4

--- a/solution.py
+++ b/solution.py
@@ -58,7 +58,7 @@
     return one_hot(row, SECTORS * LINES)
 
 
-UNROLL = 32
+UNROLL = 128
 LANES = FIELDS * ROWS * LEV
 
 
@@ -146,30 +146,29 @@
     return cosine, sine
 
 
-STEP = 16
-DEPTH = COLS + STEP
+STEP = 32
+HALVES = 2
+DEPTH = WIDE // HALVES
+TURNS = HALVES * SECTORS
 BLOCK = 256
 BLOCKS = M // BLOCK
-EARLY = 4
-AUX = 24
+AUX = 2 * TURNS + 8
 
 
 def table_kernel(points_ref, mode_ref, *refs):
-    early, (aux, table_hbm, late, sems) = refs[:EARLY], refs[EARLY:]
-    table = [*early, *[late.at[n] for n in range(BLOCKS - EARLY)]]
-    copies = []
+    *table, aux = refs
     mode = mode_ref[...].astype(F32)
 
-    def rows(count, scale, first):
-        index = lax.broadcasted_iota(jnp.int32, (count, M), 0) * scale + first
-        return sincos(index.astype(F32) * mode)
-
-    coarse_c, coarse_s = rows(DEPTH // STEP, STEP, 0)
-    fine_c, fine_s = rows(STEP, 1, -REACH)
+    def rows(count, position):
+        place = position(lax.broadcasted_iota(jnp.int32, (count, M), 0))
+        return sincos(place.astype(F32) * mode)
+
+    coarse_c, coarse_s = rows(DEPTH // STEP, lambda n: n * STEP)
+    fine_c, fine_s = rows(STEP, lambda n: n - REACH)
     factor = jnp.where(mode == 0.0, 1.0, 2.0)
     fine_c = fine_c * factor
     fine_s = fine_s * factor
-    for n in (*range(EARLY, BLOCKS), *range(EARLY)):
+    for n in range(BLOCKS):
         part = slice(n * BLOCK, (n + 1) * BLOCK)
         for a in range(DEPTH // STEP):
             c = coarse_c[a : a + 1, part]
@@ -177,46 +176,38 @@
             lines = slice(a * STEP, (a + 1) * STEP)
             table[n][lines, :BLOCK] = (c * fine_c[:, part] - s * fine_s[:, part]).astype(BF16)
             table[n][lines, BLOCK:] = (-s * fine_c[:, part] - c * fine_s[:, part]).astype(BF16)
-        if n >= EARLY:
-            copies.append(pltpu.make_async_copy(table[n], table_hbm.at[n - EARLY], sems.at[n - EARLY]))
-            copies[-1].start()
-    turn_c, turn_s = rows(SECTORS, COLS, 0)
-    aux[0:SECTORS, :] = turn_c
-    aux[SECTORS : 2 * SECTORS, :] = turn_s
-    row = lax.broadcasted_iota(jnp.int32, (AUX - 2 * SECTORS, M), 0)
-    lane = lax.broadcasted_iota(jnp.int32, (AUX - 2 * SECTORS, M), 1)
-    extra = jnp.zeros((AUX - 2 * SECTORS, M), F32)
+    turn_c, turn_s = rows(TURNS, lambda n: n % SECTORS * COLS + n // SECTORS * DEPTH)
+    aux[0:TURNS, :] = turn_c
+    aux[TURNS : 2 * TURNS, :] = turn_s
+    row = lax.broadcasted_iota(jnp.int32, (AUX - 2 * TURNS, M), 0)
+    lane = lax.broadcasted_iota(jnp.int32, (AUX - 2 * TURNS, M), 1)
+    extra = jnp.zeros((AUX - 2 * TURNS, M), F32)
     for i in range(ROWS):
         count = (points_ref[i] + 1) // 2
         high = count // 16
         value = jnp.where(lane == 0, high, jnp.where(lane == 1, count - 16 * high, 0))
         extra = extra + jnp.where(row == i, value, 0).astype(F32)
-    aux[2 * SECTORS :, :] = extra
-    for copy in copies:
-        copy.wait()
+    aux[2 * TURNS :, :] = extra
 
 
 def fourier_kernel(grid_ref, *refs):
-    early, (aux, table_hbm, out_ref, late, sem, spectra, lanes, rows) = refs[:EARLY], refs[EARLY:]
-    table = [*early, *[late.at[n] for n in range(BLOCKS - EARLY)]]
-    copy = pltpu.make_async_copy(table_hbm, late, sem)
-    copy.start()
-    data = grid_ref[...].reshape(SECTORS * LINES, WIDE)[:, :DEPTH]
+    *table, aux, out_ref, spectra, lanes, rows = refs
+    data = [grid_ref[:, :, h * DEPTH : (h + 1) * DEPTH].reshape(SECTORS * LINES, DEPTH) for h in range(HALVES)]
     for n in range(BLOCKS):
         part = slice(n * BLOCK, (n + 1) * BLOCK)
-        if n == EARLY:
-            copy.wait()
-        real = dot(data, table[n][:, :BLOCK], ((1,), (0,)))
-        imag = dot(data, table[n][:, BLOCK:], ((1,), (0,)))
         sum_r = jnp.zeros((LINES, BLOCK), F32)
         sum_i = jnp.zeros((LINES, BLOCK), F32)
-        for j in range(SECTORS):
-            c = aux[j : j + 1, part]
-            s = aux[SECTORS + j : SECTORS + j + 1, part]
-            re = real[j * LINES : (j + 1) * LINES]
-            im = imag[j * LINES : (j + 1) * LINES]
-            sum_r = sum_r + c * re + s * im
-            sum_i = sum_i + c * im - s * re
+        for h in range(HALVES):
+            real = dot(data[h], table[n][:, :BLOCK], ((1,), (0,)))
+            imag = dot(data[h], table[n][:, BLOCK:], ((1,), (0,)))
+            for j in range(SECTORS):
+                turn = h * SECTORS + j
+                c = aux[turn : turn + 1, part]
+                s = aux[TURNS + turn : TURNS + turn + 1, part]
+                re = real[j * LINES : (j + 1) * LINES]
+                im = imag[j * LINES : (j + 1) * LINES]
+                sum_r = sum_r + c * re + s * im
+                sum_i = sum_i + c * im - s * re
         for t in range(TARGETS):
             here = slice(8 * t, 8 * t + 8)
             spectra[t, :, part] = jnp.concatenate([sum_r[here], sum_i[here]], axis=0).astype(BF16)
@@ -231,7 +222,7 @@
             rows[pl.ds(t * (GROUPS + 1) + g, BANDS, stride=MSG), :] = turned[at : at + BANDS]
         limit = jnp.zeros((BANDS, 128), F32)
         if 0 < t <= ROWS:
-            limit = limit + aux[2 * SECTORS + t - 1 : 2 * SECTORS + t, 0:128]
+            limit = limit + aux[2 * TURNS + t - 1 : 2 * TURNS + t, 0:128]
         rows[pl.ds(t * (GROUPS + 1) + GROUPS, BANDS, stride=MSG), :] = limit
     out_ref[...] = rows[...].astype(BF16).reshape(out_ref.shape)
 
@@ -361,20 +352,15 @@
         cost_estimate=pl.CostEstimate(flops=20_000_000, bytes_accessed=1_500_000, transcendentals=0),
     )(*hbm(grid_cot, weights, offsets))
     column_mode = slot_mode.reshape(BANDS, GROUPS, LANE_SLOTS).transpose(2, 1, 0).reshape(1, M)
-    *tables, table_rest = pl.pallas_call(
+    tables = pl.pallas_call(
         table_kernel,
         name="table",
         out_shape=(
-            *[pltpu.VMEM((DEPTH, 2 * BLOCK), BF16)] * EARLY,
+            *[pltpu.VMEM((DEPTH, 2 * BLOCK), BF16)] * BLOCKS,
             pltpu.VMEM((AUX, M), F32),
-            pltpu.HBM((BLOCKS - EARLY, DEPTH, 2 * BLOCK), BF16),
         ),
         in_specs=[in_smem(), in_vmem()],
-        out_specs=(*[in_vmem()] * (EARLY + 1), in_hbm()),
-        scratch_shapes=[
-            pltpu.VMEM((BLOCKS - EARLY, DEPTH, 2 * BLOCK), BF16),
-            pltpu.SemaphoreType.DMA((BLOCKS - EARLY,)),
-        ],
+        out_specs=(in_vmem(),) * (BLOCKS + 1),
         compiler_params=params(12),
         cost_estimate=pl.CostEstimate(flops=20_000_000, bytes_accessed=4_000_000, transcendentals=0),
     )(lat_points, column_mode)
@@ -383,18 +369,16 @@
         fourier_kernel,
         name="fourier",
         out_shape=pltpu.VMEM((BANDS, MSG, 128), BF16),
-        in_specs=[in_vmem()] * (EARLY + 2) + [in_hbm()],
+        in_specs=[in_vmem()] * (BLOCKS + 2),
         out_specs=in_vmem(),
         scratch_shapes=[
-            pltpu.VMEM((BLOCKS - EARLY, DEPTH, 2 * BLOCK), BF16),
-            pltpu.SemaphoreType.DMA,
             pltpu.VMEM((TARGETS, 16, M), BF16),
             pltpu.VMEM((128, TARGETS * BANDS * GROUPS), BF16),
             pltpu.VMEM((BANDS * MSG, 128), F32),
         ],
         compiler_params=params(14),
         cost_estimate=pl.CostEstimate(flops=1_000_000_000, bytes_accessed=5_000_000, transcendentals=0),
-    )(circles, *vmem(*tables), *hbm(table_rest))
+    )(circles, *vmem(*tables))
     shape = (SLOTS, 2, FIELDS, PER_PEER, NL)
     message, legendre = lax.optimization_barrier((message, legendre.reshape(QUADS, 4 * NLAT, NL)))
     staged = pl.pallas_call(

time: 50.8 us -> 49.8 us (0.980)
  Pallas kernels: 16.1 us -> 14.7 us
    pallas_call x1, Pallas kernels: 3.14 us -> 2.43 us  [per_device(): pl.pallas_call(fourier_kernel, name='fourier', out_shape=pltpu.VMEM((BAND...]
  transfers between devices with their start and end apart: 2 -> 2, of which waited for: 2 -> 2; matrix products, arithmetic and copies ran while one was open for 2% -> 2% of each run, Pallas kernels for 8% -> 7%
where the time goes in v5:
time: 49.8 us; the launch traced here: 49.5 us
  starting transfers between devices  18.4 us (37%)
  Pallas kernels  14.7 us (30%)
  waiting for transfers between devices  14.6 us (29%)
  local copies, waits for them, and re-layouts  1.65 us (3%)
    all_to_all x1, starting transfers between devices, per_device(): lax.all_to_all(message, 'lat', split_axis=0, concat_axis=0, tiled=True)  12.2 us
    all_to_all x1, waiting for transfers between devices, per_device(): lax.all_to_all(message, 'lat', split_axis=0, concat_axis=0, tiled=True)  10 us
    all_to_all x1, starting transfers between devices, per_device(): lax.all_to_all(sent, 'lon', split_axis=0, concat_axis=0, tiled=True)  6.21 us
    pallas_call x1, Pallas kernels, per_device(): pl.pallas_call(legendre_kernel, name='legendre', out_shape=jax.ShapeDtype...  4.65 us
    all_to_all x1, waiting for transfers between devices, per_device(): lax.all_to_all(sent, 'lon', split_axis=0, concat_axis=0, tiled=True)  4.61 us
    pallas_call x1, Pallas kernels, per_device(): pl.pallas_call(deposit_kernel, name='deposit', out_shape=pltpu.VMEM((SECT...  4.22 us
    pallas_call x1, Pallas kernels, per_device(): pl.pallas_call(fourier_kernel, name='fourier', out_shape=pltpu.VMEM((BAND...  2.43 us
    pallas_call x1, Pallas kernels, per_device(): pl.pallas_call(stage_kernel, name='stage', out_shape=(*[pltpu.VMEM((4 * N...  1.92 us
  transfers between devices with their start and end apart: 2, of which 2 were waited for; matrix products, arithmetic and copies ran while one was open for 2% of the time, Pallas kernels for 7%

profile of v5, /device:TPU:1, one launch (start us, length us, event | category | flops | bytes accessed | tf_op | source)
XLA Modules:
  0.0 49.5 jit_solution(11108032969203110432)
XLA Ops:
  0.0 0.0 copy-start
  0.0 4.2 %deposit.1 = bf16[8,32,768]{2,1,0:T(8,128)(2,1)} custom-call(f32[4,2,16,640]{3,2,1,0:T(8,128)} %grid_hbm.1, bf16[2,16,4,640]{3,2,1,0:T(4,128)(2,1)} %weight_hbm.1, s32[2,16,2,640]{3,2,1,0:T(2,128)} %offset_hbm.1), custom_call_target="tpu_custom_call" | custom-call | flops 20000000 | bytes 1500000 | tf_op jit(solution)/shard_map/deposit/pallas_call | solution.py:334
  4.2 6.2 %all-to-all-start = ((bf16[8,32,768]{2,1,0:T(8,128)(2,1)}), bf16[8,32,768]{2,1,0:T(8,128)(2,1)S(1)}, u32[]{:S(2)}, u32[]{:S(2)}) async-start(bf16[8,32,768]{2,1,0:T(8,128)(2,1)} %deposit.1), calls=%async_computation | async-start | bytes 786432 | tf_op jit(solution)/shard_map/all_to_all | solution.py:367
  10.4 0.8 %reshape.9 = s32[32,5,8]{2,1,0:T(8,128)S(1)} reshape(s32[1280]{0:T(1024)} %mode_ref.1) | data formatting | bytes 10240 | tf_op jit(solution)/shard_map/reshape | solution.py:354
  11.2 0.1 copy.7
  11.4 0.1 reshape.10.mode_ref
  11.4 0.0 copy-start.1
  11.4 0.7 %copy-done.1 = s32[2]{0:T(128)S(1)} copy-done((s32[2]{0:T(128)S(1)}, s32[2]{0:T(128)}, u32[]{:S(2)}) %copy-start.1) | copy-done | bytes 32
  12.1 1.5 %table.1 = (bf16[384,512]{1,0:T(8,128)(2,1)S(1)}, bf16[384,512]{1,0:T(8,128)(2,1)S(1)}, bf16[384,512]{1,0:T(8,128)(2,1)S(1)}, bf16[384,512]{1,0:T(8,128)(2,1)S(1...) custom-call(s32[2]{0:T(128)S(1)} %copy-done.1, s32[1,1280]{1,0:T(1,128)S(1)} %reshape.10.mode_ref), custom_call_target="tpu_custom_call" | custom-call | flops 20000000 | bytes 4000000 | tf_op jit(solution)/shard_map/table/pallas_call | solution.py:355
  13.6 4.6 %all-to-all-done.grid_ref = bf16[8,32,768]{2,1,0:T(8,128)(2,1)S(1)} async-done(((bf16[8,32,768]{2,1,0:T(8,128)(2,1)}), bf16[8,32,768]{2,1,0:T(8,128)(2,1)S(1)}, u32[]{:S(2)}, u32[]{:S(2)}) %all-to-all-start) | async-done | bytes 393248 | tf_op jit(solution)/shard_map/all_to_all | solution.py:367
  18.2 2.4 %fourier.1 = bf16[32,24,128]{2,1,0:T(8,128)(2,1)} custom-call(bf16[8,32,768]{2,1,0:T(8,128)(2,1)S(1)} %all-to-all-done.grid_ref, bf16[384,512]{1,0:T(8,128)(2,1)S(1)} %get-tuple-element.18.refs_0_, bf16[384,512]{1,0:T(8,128)(2,1)S(1)} %get-tuple-element.19.refs_1_, bf16[384,512]{1,0:T(8,128)(2,1)S(1)} %get-tuple-element.20.refs_2_, ...), custom_call_target="tpu_custom_call" | custom-call | flops 1000000000 | bytes 5000000 | tf_op jit(solution)/shard_map/fourier/pallas_call | solution.py:368
  20.7 12.2 %all-to-all-start.1 = ((bf16[32,24,128]{2,1,0:T(8,128)(2,1)}), bf16[32,24,128]{2,1,0:T(8,128)(2,1)S(1)}, u32[]{:S(2)}, u32[]{:S(2)}) async-start(bf16[32,24,128]{2,1,0:T(8,128)(2,1)} %fourier.1), calls=%async_computation.1 | async-start | bytes 393216 | tf_op jit(solution)/shard_map/all_to_all | solution.py:396
  32.9 1.9 %stage.1 = (bf16[256,1280]{1,0:T(8,128)(2,1)S(1)}, bf16[256,1280]{1,0:T(8,128)(2,1)S(1)}, bf16[256,1280]{1,0:T(8,128)(2,1)S(1)}, bf16[256,1280]{1,0:T(8,128)(2,1)S(1)}, bf16[256,1280]{1,0:T(8,128)(2,1)S(1)}) custom-call(bf16[10,256,1280]{2,1,0:T(8,128)(2,1)} %bitcast.2), custom_call_target="tpu_custom_call" | custom-call | bytes 16000000 | tf_op jit(solution)/shard_map/stage/pallas_call | solution.py:384
  34.8 10.0 %all-to-all-done.1.msg_ref = bf16[32,24,128]{2,1,0:T(8,128)(2,1)S(1)} async-done(((bf16[32,24,128]{2,1,0:T(8,128)(2,1)}), bf16[32,24,128]{2,1,0:T(8,128)(2,1)S(1)}, u32[]{:S(2)}, u32[]{:S(2)}) %all-to-all-start.1) | async-done | bytes 196640 | tf_op jit(solution)/shard_map/all_to_all | solution.py:396
  44.8 0.0 copy-done
  44.8 4.6 %legendre.1 = bf16[40,2,4,2,1280]{4,3,2,1,0:T(2,128)(2,1)} custom-call(s32[1280]{0:T(1024)S(1)} %copy-done, bf16[32,24,128]{2,1,0:T(8,128)(2,1)S(1)} %all-to-all-done.1.msg_ref, bf16[256,1280]{1,0:T(8,128)(2,1)S(1)} %get-tuple-element.26.refs_0_, bf16[256,1280]{1,0:T(8,128)(2,1)S(1)} %get-tuple-element.27.refs_1_, ...), custom_call_target="tpu_custom_call" | custom-call | flops 500000000 | bytes 8000000 | tf_op jit(solution)/shard_map/legendre/pallas_call | solution.py:397
Async XLA Ops:
  0.0 44.8 %copy-start = (s32[1280]{0:T(1024)S(1)}, s32[1280]{0:T(1024)}, u32[]{:S(2)}) copy-start(s32[1280]{0:T(1024)} %mode_ref.1) | copy-start | bytes 15364
  4.2 14.0 %all-to-all-start = ((bf16[8,32,768]{2,1,0:T(8,128)(2,1)}), bf16[8,32,768]{2,1,0:T(8,128)(2,1)S(1)}, u32[]{:S(2)}, u32[]{:S(2)}) async-start(bf16[8,32,768]{2,1,0:T(8,128)(2,1)} %deposit.1), calls=%async_computation | async-start | bytes 786432 | tf_op jit(solution)/shard_map/all_to_all | solution.py:367
  11.4 0.7 %copy-start.1 = (s32[2]{0:T(128)S(1)}, s32[2]{0:T(128)}, u32[]{:S(2)}) copy-start(s32[2]{0:T(128)} %points_ref.1) | copy-start | bytes 28
  20.7 24.2 %all-to-all-start.1 = ((bf16[32,24,128]{2,1,0:T(8,128)(2,1)}), bf16[32,24,128]{2,1,0:T(8,128)(2,1)S(1)}, u32[]{:S(2)}, u32[]{:S(2)}) async-start(bf16[32,24,128]{2,1,0:T(8,128)(2,1)} %fourier.1), calls=%async_computation.1 | async-start | bytes 393216 | tf_op jit(solution)/shard_map/all_to_all | solution.py:396

commit v6 on v5

--- a/solution.py
+++ b/solution.py
@@ -224,7 +224,7 @@
         if 0 < t <= ROWS:
             limit = limit + aux[2 * TURNS + t - 1 : 2 * TURNS + t, 0:128]
         rows[pl.ds(t * (GROUPS + 1) + GROUPS, BANDS, stride=MSG), :] = limit
-    out_ref[...] = rows[...].astype(BF16).reshape(out_ref.shape)
+    out_ref[...] = rows[: BANDS * MSG].astype(BF16).reshape(out_ref.shape)
 
 
 QUADS = SLOTS // 4
@@ -255,7 +255,7 @@
     base = lax.axis_index("lat") * SLOTS
     rows[0:MSG] = jnp.zeros((MSG, 128), F32)
     rows[MSG : (BANDS + 1) * MSG] = msg_ref[...].reshape(BANDS * MSG, 128).astype(F32)
-    rows[(BANDS + 1) * MSG :] = jnp.zeros((MSG, 128), F32)
+    rows[(BANDS + 1) * MSG :] = jnp.zeros((2 * MSG, 128), F32)
     for g in range(GROUPS + 1):
 
         def part(t, neighbour):
@@ -263,7 +263,7 @@
 
         mixed[pl.ds(g * NLAT, BANDS, stride=2), :] = part(1, 0) + part(3, -1)
         mixed[pl.ds(g * NLAT + 1, BANDS, stride=2), :] = part(2, 0) + part(0, 1)
-    spread = mixed[...].T
+    spread = mixed[: (GROUPS + 1) * NLAT].T
     lane = lax.broadcasted_iota(jnp.int32, (16, 128), 1)
     first = lane < NLAT
     plain = [spread[:, 128 * p : 128 * p + 128] for p in range((GROUPS + 1) // 2)]
@@ -374,7 +374,7 @@
         scratch_shapes=[
             pltpu.VMEM((TARGETS, 16, M), BF16),
             pltpu.VMEM((128, TARGETS * BANDS * GROUPS), BF16),
-            pltpu.VMEM((BANDS * MSG, 128), F32),
+            pltpu.VMEM(((BANDS + 1) * MSG, 128), F32),
         ],
         compiler_params=params(14),
         cost_estimate=pl.CostEstimate(flops=1_000_000_000, bytes_accessed=5_000_000, transcendentals=0),
@@ -405,8 +405,8 @@
             pltpu.VMEM(shape, BF16),
             pltpu.SemaphoreType.DMA((2,)),
             pltpu.SemaphoreType.DMA((QUADS,)),
-            pltpu.VMEM(((BANDS + 2) * MSG, 128), F32),
-            pltpu.VMEM(((GROUPS + 1) * NLAT, 128), F32),
+            pltpu.VMEM(((BANDS + 3) * MSG, 128), F32),
+            pltpu.VMEM(((GROUPS + 1) * NLAT + 8, 128), F32),
         ],
         compiler_params=params(12),
         cost_estimate=pl.CostEstimate(flops=500_000_000, bytes_accessed=8_000_000, transcendentals=0),

time: 49.8 us -> 49.8 us (level)
  no operation moved by 1% of the time
where the time goes in v6:
time: 49.8 us; the launch traced here: 49.5 us
  starting transfers between devices  18.4 us (37%)
  Pallas kernels  14.7 us (30%)
  waiting for transfers between devices  14.6 us (29%)
  local copies, waits for them, and re-layouts  1.65 us (3%)
    all_to_all x1, starting transfers between devices, per_device(): lax.all_to_all(message, 'lat', split_axis=0, concat_axis=0, tiled=True)  12.2 us
    all_to_all x1, waiting for transfers between devices, per_device(): lax.all_to_all(message, 'lat', split_axis=0, concat_axis=0, tiled=True)  10 us
    all_to_all x1, starting transfers between devices, per_device(): lax.all_to_all(sent, 'lon', split_axis=0, concat_axis=0, tiled=True)  6.21 us
    pallas_call x1, Pallas kernels, per_device(): pl.pallas_call(legendre_kernel, name='legendre', out_shape=jax.ShapeDtype...  4.65 us
    all_to_all x1, waiting for transfers between devices, per_device(): lax.all_to_all(sent, 'lon', split_axis=0, concat_axis=0, tiled=True)  4.61 us
    pallas_call x1, Pallas kernels, per_device(): pl.pallas_call(deposit_kernel, name='deposit', out_shape=pltpu.VMEM((SECT...  4.22 us
    pallas_call x1, Pallas kernels, per_device(): pl.pallas_call(fourier_kernel, name='fourier', out_shape=pltpu.VMEM((BAND...  2.43 us
    pallas_call x1, Pallas kernels, per_device(): pl.pallas_call(stage_kernel, name='stage', out_shape=(*[pltpu.VMEM((4 * N...  1.92 us
  transfers between devices with their start and end apart: 2, of which 2 were waited for; matrix products, arithmetic and copies ran while one was open for 2% of the time, Pallas kernels for 7%

profile of v6, /device:TPU:1, one launch (start us, length us, event | category | flops | bytes accessed | tf_op | source)
XLA Modules:
  0.0 49.5 jit_solution(3800386462883925824)
XLA Ops:
  0.0 0.0 copy-start
  0.0 4.2 %deposit.1 = bf16[8,32,768]{2,1,0:T(8,128)(2,1)} custom-call(f32[4,2,16,640]{3,2,1,0:T(8,128)} %grid_hbm.1, bf16[2,16,4,640]{3,2,1,0:T(4,128)(2,1)} %weight_hbm.1, s32[2,16,2,640]{3,2,1,0:T(2,128)} %offset_hbm.1), custom_call_target="tpu_custom_call" | custom-call | flops 20000000 | bytes 1500000 | tf_op jit(solution)/shard_map/deposit/pallas_call | solution.py:334
  4.2 6.2 %all-to-all-start = ((bf16[8,32,768]{2,1,0:T(8,128)(2,1)}), bf16[8,32,768]{2,1,0:T(8,128)(2,1)S(1)}, u32[]{:S(2)}, u32[]{:S(2)}) async-start(bf16[8,32,768]{2,1,0:T(8,128)(2,1)} %deposit.1), calls=%async_computation | async-start | bytes 786432 | tf_op jit(solution)/shard_map/all_to_all | solution.py:367
  10.4 0.8 %reshape.9 = s32[32,5,8]{2,1,0:T(8,128)S(1)} reshape(s32[1280]{0:T(1024)} %mode_ref.1) | data formatting | bytes 10240 | tf_op jit(solution)/shard_map/reshape | solution.py:354
  11.2 0.1 copy.7
  11.4 0.1 reshape.10.mode_ref
  11.4 0.0 copy-start.1
  11.4 0.7 %copy-done.1 = s32[2]{0:T(128)S(1)} copy-done((s32[2]{0:T(128)S(1)}, s32[2]{0:T(128)}, u32[]{:S(2)}) %copy-start.1) | copy-done | bytes 32
  12.1 1.5 %table.1 = (bf16[384,512]{1,0:T(8,128)(2,1)S(1)}, bf16[384,512]{1,0:T(8,128)(2,1)S(1)}, bf16[384,512]{1,0:T(8,128)(2,1)S(1)}, bf16[384,512]{1,0:T(8,128)(2,1)S(1...) custom-call(s32[2]{0:T(128)S(1)} %copy-done.1, s32[1,1280]{1,0:T(1,128)S(1)} %reshape.10.mode_ref), custom_call_target="tpu_custom_call" | custom-call | flops 20000000 | bytes 4000000 | tf_op jit(solution)/shard_map/table/pallas_call | solution.py:355
  13.6 4.6 %all-to-all-done.grid_ref = bf16[8,32,768]{2,1,0:T(8,128)(2,1)S(1)} async-done(((bf16[8,32,768]{2,1,0:T(8,128)(2,1)}), bf16[8,32,768]{2,1,0:T(8,128)(2,1)S(1)}, u32[]{:S(2)}, u32[]{:S(2)}) %all-to-all-start) | async-done | bytes 393248 | tf_op jit(solution)/shard_map/all_to_all | solution.py:367
  18.2 2.4 %fourier.1 = bf16[32,24,128]{2,1,0:T(8,128)(2,1)} custom-call(bf16[8,32,768]{2,1,0:T(8,128)(2,1)S(1)} %all-to-all-done.grid_ref, bf16[384,512]{1,0:T(8,128)(2,1)S(1)} %get-tuple-element.18.refs_0_, bf16[384,512]{1,0:T(8,128)(2,1)S(1)} %get-tuple-element.19.refs_1_, bf16[384,512]{1,0:T(8,128)(2,1)S(1)} %get-tuple-element.20.refs_2_, ...), custom_call_target="tpu_custom_call" | custom-call | flops 1000000000 | bytes 5000000 | tf_op jit(solution)/shard_map/fourier/pallas_call | solution.py:368
  20.7 12.2 %all-to-all-start.1 = ((bf16[32,24,128]{2,1,0:T(8,128)(2,1)}), bf16[32,24,128]{2,1,0:T(8,128)(2,1)S(1)}, u32[]{:S(2)}, u32[]{:S(2)}) async-start(bf16[32,24,128]{2,1,0:T(8,128)(2,1)} %fourier.1), calls=%async_computation.1 | async-start | bytes 393216 | tf_op jit(solution)/shard_map/all_to_all | solution.py:396
  32.9 1.9 %stage.1 = (bf16[256,1280]{1,0:T(8,128)(2,1)S(1)}, bf16[256,1280]{1,0:T(8,128)(2,1)S(1)}, bf16[256,1280]{1,0:T(8,128)(2,1)S(1)}, bf16[256,1280]{1,0:T(8,128)(2,1)S(1)}, bf16[256,1280]{1,0:T(8,128)(2,1)S(1)}) custom-call(bf16[10,256,1280]{2,1,0:T(8,128)(2,1)} %bitcast.2), custom_call_target="tpu_custom_call" | custom-call | bytes 16000000 | tf_op jit(solution)/shard_map/stage/pallas_call | solution.py:384
  34.8 10.0 %all-to-all-done.1.msg_ref = bf16[32,24,128]{2,1,0:T(8,128)(2,1)S(1)} async-done(((bf16[32,24,128]{2,1,0:T(8,128)(2,1)}), bf16[32,24,128]{2,1,0:T(8,128)(2,1)S(1)}, u32[]{:S(2)}, u32[]{:S(2)}) %all-to-all-start.1) | async-done | bytes 196640 | tf_op jit(solution)/shard_map/all_to_all | solution.py:396
  44.8 0.0 copy-done
  44.9 4.6 %legendre.1 = bf16[40,2,4,2,1280]{4,3,2,1,0:T(2,128)(2,1)} custom-call(s32[1280]{0:T(1024)S(1)} %copy-done, bf16[32,24,128]{2,1,0:T(8,128)(2,1)S(1)} %all-to-all-done.1.msg_ref, bf16[256,1280]{1,0:T(8,128)(2,1)S(1)} %get-tuple-element.26.refs_0_, bf16[256,1280]{1,0:T(8,128)(2,1)S(1)} %get-tuple-element.27.refs_1_, ...), custom_call_target="tpu_custom_call" | custom-call | flops 500000000 | bytes 8000000 | tf_op jit(solution)/shard_map/legendre/pallas_call | solution.py:397
Async XLA Ops:
  0.0 44.8 %copy-start = (s32[1280]{0:T(1024)S(1)}, s32[1280]{0:T(1024)}, u32[]{:S(2)}) copy-start(s32[1280]{0:T(1024)} %mode_ref.1) | copy-start | bytes 15364
  4.2 14.0 %all-to-all-start = ((bf16[8,32,768]{2,1,0:T(8,128)(2,1)}), bf16[8,32,768]{2,1,0:T(8,128)(2,1)S(1)}, u32[]{:S(2)}, u32[]{:S(2)}) async-start(bf16[8,32,768]{2,1,0:T(8,128)(2,1)} %deposit.1), calls=%async_computation | async-start | bytes 786432 | tf_op jit(solution)/shard_map/all_to_all | solution.py:367
  11.4 0.7 %copy-start.1 = (s32[2]{0:T(128)S(1)}, s32[2]{0:T(128)}, u32[]{:S(2)}) copy-start(s32[2]{0:T(128)} %points_ref.1) | copy-start | bytes 28
  20.7 24.2 %all-to-all-start.1 = ((bf16[32,24,128]{2,1,0:T(8,128)(2,1)}), bf16[32,24,128]{2,1,0:T(8,128)(2,1)S(1)}, u32[]{:S(2)}, u32[]{:S(2)}) async-start(bf16[32,24,128]{2,1,0:T(8,128)(2,1)} %fourier.1), calls=%async_computation.1 | async-start | bytes 393216 | tf_op jit(solution)/shard_map/all_to_all | solution.py:396

commit v7 on v6

--- a/solution.py
+++ b/solution.py
@@ -63,18 +63,22 @@
 
 
 def deposit_kernel(
-    grid_hbm, weight_hbm, offset_hbm, out_ref, grid, weight, offset, sems, stacked, wide, terms, sums, parts
+    grid_hbm, weight_hbm, offset_hbm, out_ref, grid, weight, offset, sems, stacked, wide, terms, sums, parts, spread, order
 ):
     pairs = ((offset_hbm, offset), (weight_hbm, weight), (grid_hbm, grid))
     copies = [pltpu.make_async_copy(src, dst, sems.at[n]) for n, (src, dst) in enumerate(pairs)]
     for copy in copies:
         copy.start()
-    spread = spread_order()
-    order = line_order()
-    for n in range(7):
-        fill = jnp.full((8, LANES), 99.0 if n == 0 else 0.0, F32)
-        terms[n, 0:8] = fill
-        terms[n, COLS + 8 : COLS + 16] = fill
+
+    @pl.when(lax.axis_index("lat") >= 0)
+    def _():
+        spread[...] = spread_order()
+        order[...] = line_order()
+        for n in range(7):
+            fill = jnp.full((8, LANES), 99.0 if n == 0 else 0.0, F32)
+            terms[n, 0:8] = fill
+            terms[n, COLS + 8 : COLS + 16] = fill
+
     copies[0].wait()
     for i in range(ROWS):
         for v in range(LEV):
@@ -85,7 +89,7 @@
         for v in range(LEV):
             at = (i * LEV + v) * 4
             stacked[at : at + 4, :] = weight[i, v].astype(F32)
-    wide[...] = dot(stacked[...].astype(BF16), spread, ((0,), (0,)))
+    wide[...] = dot(stacked[...].astype(BF16), spread[...], ((0,), (0,)))
     copies[2].wait()
     for j in range(COLS // 128):
         rows = slice(128 * j, 128 * j + 128)
@@ -127,7 +131,7 @@
     inner = lax.broadcasted_iota(jnp.int32, (1, LANES), 1) < FIELDS * LEV
     parts[:, :LANES] = jnp.where(inner, north, south).astype(BF16)
     parts[:, LANES:] = (same + pltpu.roll(jnp.where(inner, south, north), FIELDS * LEV, 1)).astype(BF16)
-    ordered = dot(order, parts[...], ((1,), (1,)))
+    ordered = dot(order[...], parts[...], ((1,), (1,)))
     out_ref[...] = ordered.astype(BF16).reshape(out_ref.shape)
 
 
@@ -347,6 +351,8 @@
             pltpu.VMEM((7, COLS + 16, LANES), F32),
             pltpu.VMEM((3, WIDE, LANES), F32),
             pltpu.VMEM((WIDE, 2 * LANES), BF16),
+            pltpu.VMEM((6 * ROWS * LEV, 6 * LANES), BF16),
+            pltpu.VMEM((SECTORS * LINES, 2 * LANES), BF16),
         ],
         compiler_params=params(14),
         cost_estimate=pl.CostEstimate(flops=20_000_000, bytes_accessed=1_500_000, transcendentals=0),

time: 49.8 us -> 49.8 us (level)
  no operation moved by 1% of the time
where the time goes in v7:
time: 49.8 us; the launch traced here: 49.5 us
  starting transfers between devices  18.4 us (37%)
  Pallas kernels  14.7 us (30%)
  waiting for transfers between devices  14.6 us (29%)
  local copies, waits for them, and re-layouts  1.65 us (3%)
    all_to_all x1, starting transfers between devices, per_device(): lax.all_to_all(message, 'lat', split_axis=0, concat_axis=0, tiled=True)  12.2 us
    all_to_all x1, waiting for transfers between devices, per_device(): lax.all_to_all(message, 'lat', split_axis=0, concat_axis=0, tiled=True)  10 us
    all_to_all x1, starting transfers between devices, per_device(): lax.all_to_all(sent, 'lon', split_axis=0, concat_axis=0, tiled=True)  6.21 us
    pallas_call x1, Pallas kernels, per_device(): pl.pallas_call(legendre_kernel, name='legendre', out_shape=jax.ShapeDtype...  4.65 us
    all_to_all x1, waiting for transfers between devices, per_device(): lax.all_to_all(sent, 'lon', split_axis=0, concat_axis=0, tiled=True)  4.61 us
    pallas_call x1, Pallas kernels, per_device(): pl.pallas_call(deposit_kernel, name='deposit', out_shape=pltpu.VMEM((SECT...  4.22 us
    pallas_call x1, Pallas kernels, per_device(): pl.pallas_call(fourier_kernel, name='fourier', out_shape=pltpu.VMEM((BAND...  2.43 us
    pallas_call x1, Pallas kernels, per_device(): pl.pallas_call(stage_kernel, name='stage', out_shape=(*[pltpu.VMEM((4 * N...  1.92 us
  transfers between devices with their start and end apart: 2, of which 2 were waited for; matrix products, arithmetic and copies ran while one was open for 2% of the time, Pallas kernels for 7%

profile of v7, /device:TPU:1, one launch (start us, length us, event | category | flops | bytes accessed | tf_op | source)
XLA Modules:
  0.0 49.5 jit_solution(17680915229960918256)
XLA Ops:
  0.0 0.0 copy-start
  0.0 4.2 %deposit.1 = bf16[8,32,768]{2,1,0:T(8,128)(2,1)} custom-call(f32[4,2,16,640]{3,2,1,0:T(8,128)} %grid_hbm.1, bf16[2,16,4,640]{3,2,1,0:T(4,128)(2,1)} %weight_hbm.1, s32[2,16,2,640]{3,2,1,0:T(2,128)} %offset_hbm.1), custom_call_target="tpu_custom_call" | custom-call | flops 20000000 | bytes 1500000 | tf_op jit(solution)/shard_map/deposit/pallas_call | solution.py:338
  4.2 6.2 %all-to-all-start = ((bf16[8,32,768]{2,1,0:T(8,128)(2,1)}), bf16[8,32,768]{2,1,0:T(8,128)(2,1)S(1)}, u32[]{:S(2)}, u32[]{:S(2)}) async-start(bf16[8,32,768]{2,1,0:T(8,128)(2,1)} %deposit.1), calls=%async_computation | async-start | bytes 786432 | tf_op jit(solution)/shard_map/all_to_all | solution.py:373
  10.4 0.8 %reshape.9 = s32[32,5,8]{2,1,0:T(8,128)S(1)} reshape(s32[1280]{0:T(1024)} %mode_ref.1) | data formatting | bytes 10240 | tf_op jit(solution)/shard_map/reshape | solution.py:360
  11.2 0.1 copy.7
  11.3 0.1 reshape.10.mode_ref
  11.4 0.0 copy-start.1
  11.4 0.7 %copy-done.1 = s32[2]{0:T(128)S(1)} copy-done((s32[2]{0:T(128)S(1)}, s32[2]{0:T(128)}, u32[]{:S(2)}) %copy-start.1) | copy-done | bytes 32
  12.1 1.5 %table.1 = (bf16[384,512]{1,0:T(8,128)(2,1)S(1)}, bf16[384,512]{1,0:T(8,128)(2,1)S(1)}, bf16[384,512]{1,0:T(8,128)(2,1)S(1)}, bf16[384,512]{1,0:T(8,128)(2,1)S(1...) custom-call(s32[2]{0:T(128)S(1)} %copy-done.1, s32[1,1280]{1,0:T(1,128)S(1)} %reshape.10.mode_ref), custom_call_target="tpu_custom_call" | custom-call | flops 20000000 | bytes 4000000 | tf_op jit(solution)/shard_map/table/pallas_call | solution.py:361
  13.6 4.6 %all-to-all-done.grid_ref = bf16[8,32,768]{2,1,0:T(8,128)(2,1)S(1)} async-done(((bf16[8,32,768]{2,1,0:T(8,128)(2,1)}), bf16[8,32,768]{2,1,0:T(8,128)(2,1)S(1)}, u32[]{:S(2)}, u32[]{:S(2)}) %all-to-all-start) | async-done | bytes 393248 | tf_op jit(solution)/shard_map/all_to_all | solution.py:373
  18.2 2.4 %fourier.1 = bf16[32,24,128]{2,1,0:T(8,128)(2,1)} custom-call(bf16[8,32,768]{2,1,0:T(8,128)(2,1)S(1)} %all-to-all-done.grid_ref, bf16[384,512]{1,0:T(8,128)(2,1)S(1)} %get-tuple-element.18.refs_0_, bf16[384,512]{1,0:T(8,128)(2,1)S(1)} %get-tuple-element.19.refs_1_, bf16[384,512]{1,0:T(8,128)(2,1)S(1)} %get-tuple-element.20.refs_2_, ...), custom_call_target="tpu_custom_call" | custom-call | flops 1000000000 | bytes 5000000 | tf_op jit(solution)/shard_map/fourier/pallas_call | solution.py:374
  20.7 12.2 %all-to-all-start.1 = ((bf16[32,24,128]{2,1,0:T(8,128)(2,1)}), bf16[32,24,128]{2,1,0:T(8,128)(2,1)S(1)}, u32[]{:S(2)}, u32[]{:S(2)}) async-start(bf16[32,24,128]{2,1,0:T(8,128)(2,1)} %fourier.1), calls=%async_computation.1 | async-start | bytes 393216 | tf_op jit(solution)/shard_map/all_to_all | solution.py:402
  32.9 1.9 %stage.1 = (bf16[256,1280]{1,0:T(8,128)(2,1)S(1)}, bf16[256,1280]{1,0:T(8,128)(2,1)S(1)}, bf16[256,1280]{1,0:T(8,128)(2,1)S(1)}, bf16[256,1280]{1,0:T(8,128)(2,1)S(1)}, bf16[256,1280]{1,0:T(8,128)(2,1)S(1)}) custom-call(bf16[10,256,1280]{2,1,0:T(8,128)(2,1)} %bitcast.2), custom_call_target="tpu_custom_call" | custom-call | bytes 16000000 | tf_op jit(solution)/shard_map/stage/pallas_call | solution.py:390
  34.8 10.0 %all-to-all-done.1.msg_ref = bf16[32,24,128]{2,1,0:T(8,128)(2,1)S(1)} async-done(((bf16[32,24,128]{2,1,0:T(8,128)(2,1)}), bf16[32,24,128]{2,1,0:T(8,128)(2,1)S(1)}, u32[]{:S(2)}, u32[]{:S(2)}) %all-to-all-start.1) | async-done | bytes 196640 | tf_op jit(solution)/shard_map/all_to_all | solution.py:402
  44.9 0.0 copy-done
  44.9 4.7 %legendre.1 = bf16[40,2,4,2,1280]{4,3,2,1,0:T(2,128)(2,1)} custom-call(s32[1280]{0:T(1024)S(1)} %copy-done, bf16[32,24,128]{2,1,0:T(8,128)(2,1)S(1)} %all-to-all-done.1.msg_ref, bf16[256,1280]{1,0:T(8,128)(2,1)S(1)} %get-tuple-element.26.refs_0_, bf16[256,1280]{1,0:T(8,128)(2,1)S(1)} %get-tuple-element.27.refs_1_, ...), custom_call_target="tpu_custom_call" | custom-call | flops 500000000 | bytes 8000000 | tf_op jit(solution)/shard_map/legendre/pallas_call | solution.py:403
Async XLA Ops:
  0.0 44.9 %copy-start = (s32[1280]{0:T(1024)S(1)}, s32[1280]{0:T(1024)}, u32[]{:S(2)}) copy-start(s32[1280]{0:T(1024)} %mode_ref.1) | copy-start | bytes 15364
  4.2 14.0 %all-to-all-start = ((bf16[8,32,768]{2,1,0:T(8,128)(2,1)}), bf16[8,32,768]{2,1,0:T(8,128)(2,1)S(1)}, u32[]{:S(2)}, u32[]{:S(2)}) async-start(bf16[8,32,768]{2,1,0:T(8,128)(2,1)} %deposit.1), calls=%async_computation | async-start | bytes 786432 | tf_op jit(solution)/shard_map/all_to_all | solution.py:373
  11.4 0.7 %copy-start.1 = (s32[2]{0:T(128)S(1)}, s32[2]{0:T(128)}, u32[]{:S(2)}) copy-start(s32[2]{0:T(128)} %points_ref.1) | copy-start | bytes 28
  20.7 24.2 %all-to-all-start.1 = ((bf16[32,24,128]{2,1,0:T(8,128)(2,1)}), bf16[32,24,128]{2,1,0:T(8,128)(2,1)S(1)}, u32[]{:S(2)}, u32[]{:S(2)}) async-start(bf16[32,24,128]{2,1,0:T(8,128)(2,1)} %fourier.1), calls=%async_computation.1 | async-start | bytes 393216 | tf_op jit(solution)/shard_map/all_to_all | solution.py:402
